TPU v7x, 512 devices: a whole 4x4x16 slice. The times are simulated.
512 devices in a mesh: seq: 64 (over y, z), kv: 8 (over x, core).
Axes of the slice: x: 4, y: 4, z: 16, core: 2. Of those that a mesh axis runs over, the one named last changes fastest.
Arguments:
- q_heads: bfloat16 [16384, 64, 128], P(('seq', 'kv')), may hold values from -21 to 21
- k_heads: bfloat16 [16384, 8, 128], P(('seq', 'kv')), may hold values from -10 to 10
- v_heads: bfloat16 [16384, 8, 128], P(('seq', 'kv')), may hold values from -6 to 6
- d_out: bfloat16 [16384, 64, 128], P(('seq', 'kv')), may hold values from -6 to 6
- positions: int32 [16384], P(('seq', 'kv')), may hold values from 0 to 767, as said below
- subtree_end: int32 [16384], replicated, may hold values from 0 to 16383, as said below
- ancestors: int32 [128, 6], P('seq'), may hold values from -1 to 127, as said below
Outputs:
- attn_out: bfloat16 [16384, 64, 128], P(('seq', 'kv'))
- dq_grad: bfloat16 [16384, 64, 128], P(('seq', 'kv'))
- dk_grad: bfloat16 [16384, 8, 128], P(('seq', 'kv'))
- dv_grad: bfloat16 [16384, 8, 128], P(('seq', 'kv'))
Inputs may be any that keep to these rules, and one draw needn't show every extreme that they name: `ancestors`: row b lists the blocks on the path from the root of b's prefix tree down to b itself, root first, then -1 to the end of the row. The blocks of one tree are consecutive, at most 15 of them, so every listed block lies in b - 14 to b. Tokens stand in depth-first order of a forest of prefix trees; key s is an ancestor of query t, or t itself, exactly when s <= t <= subtree_end[s]. The first token of every block is an ancestor of all later tokens of its block and of all tokens of the blocks below it. `positions`: each token's depth in its prefix tree, 0 at the first token of a tree.
All inputs are finite; a program needn't handle non-finite values.
Results may differ from a plain program's by a relative error of at most 0.02.
Values may be sent and summed in bfloat16 or wider, within the bound.
A program may use at most 64 MiB of HBM per device.

v0:
```python
import math

import jax
import jax.numpy as jnp
from jax import lax
from jax.sharding import PartitionSpec as P

BLK = 128
WIN = 7


rope_base = 500000.0
masked_value = -1e30


def from_behind(value, axis, steps):
    count = lax.axis_size(axis)
    initial, last = (max(0, -steps), min(count, count - steps))
    return lax.ppermute(value, axis, [(source, source + steps) for source in range(initial, last)])


def rope_tables(positions, head_width):
    half_width = head_width // 2
    exponent = jnp.arange(half_width, dtype=jnp.float32) * (2.0 / head_width)
    frequency = jnp.power(jnp.float32(rope_base), -exponent)
    angle = positions.astype(jnp.float32)[:, None] * frequency[None, :]
    cosine = jnp.concatenate([jnp.cos(angle), jnp.cos(angle)], axis=1)[:, None, :]
    sine = jnp.concatenate([jnp.sin(angle), jnp.sin(angle)], axis=1)[:, None, :]
    return (cosine, sine)


def rotate_half(values):
    half_width = values.shape[-1] // 2
    return jnp.concatenate([-values[..., half_width:], values[..., :half_width]], axis=-1)


def rope_apply(values, cosine, sine):
    return values * cosine + rotate_half(values) * sine


def rope_back(values, cosine, sine):
    return values * cosine - rotate_half(values) * sine


def widen(values):
    return lax.optimization_barrier(values).astype(jnp.float32)


def body(q_heads, k_heads, v_heads, d_out, positions, subtree_end, ancestors):
    head_width = q_heads.shape[2]
    score_scale = 1.0 / math.sqrt(head_width)
    cosine, sine = rope_tables(positions, head_width)
    q_rot = rope_apply(q_heads.astype(jnp.float32), cosine, sine).astype(jnp.bfloat16)
    k_rot = rope_apply(k_heads.astype(jnp.float32), cosine, sine).astype(jnp.bfloat16)
    q_local, grad_local, k_local, v_local = (
        lax.all_to_all(q_rot, "kv", split_axis=1, concat_axis=0, tiled=True),
        lax.all_to_all(d_out, "kv", split_axis=1, concat_axis=0, tiled=True),
        lax.all_to_all(k_rot, "kv", split_axis=1, concat_axis=0, tiled=True),
        lax.all_to_all(v_heads, "kv", split_axis=1, concat_axis=0, tiled=True),
    )
    tok_dev = q_local.shape[0]
    kv_local = k_local.shape[1]
    group_size = q_local.shape[1] // kv_local
    blocks_here = tok_dev // BLK
    seq_index = lax.axis_index("seq")
    kv_pair = jnp.stack([k_local, v_local])
    pieces = [kv_pair]
    for offset in range(1, WIN + 1):
        pieces.insert(0, from_behind(kv_pair, "seq", offset))
    window = jnp.concatenate(pieces, axis=1)
    key_window = window[0]
    value_window = window[1]
    window_rows = key_window.shape[0]
    window_first = (seq_index - WIN) * blocks_here
    inside = jnp.arange(BLK, dtype=jnp.int32)
    key_grad = jnp.zeros((window_rows, kv_local, head_width), jnp.float32)
    value_grad = jnp.zeros((window_rows, kv_local, head_width), jnp.float32)
    stats_shape = (kv_local, group_size, BLK)
    out_blocks = []
    query_blocks = []
    for local_block in range(blocks_here):
        queries = lax.slice_in_dim(
            q_local, local_block * BLK, (local_block + 1) * BLK, axis=0
        ).reshape(BLK, kv_local, group_size, head_width)
        grad_rows = lax.slice_in_dim(
            grad_local, local_block * BLK, (local_block + 1) * BLK, axis=0
        ).reshape(BLK, kv_local, group_size, head_width)
        listed = ancestors[local_block]
        listed_count = jnp.sum((listed >= 0).astype(jnp.int32))
        query_pos = (seq_index * blocks_here + local_block) * BLK + inside

        def block_terms(listed_slot, queries=queries, listed=listed, query_pos=query_pos):
            ancestor = listed[listed_slot]
            row_start = (ancestor - window_first) * BLK
            key_rows = lax.dynamic_slice_in_dim(key_window, row_start, BLK, 0)
            value_rows = lax.dynamic_slice_in_dim(value_window, row_start, BLK, 0)
            key_end = lax.dynamic_slice_in_dim(subtree_end, ancestor * BLK, BLK, 0)
            key_pos = ancestor * BLK + inside
            visible = (key_pos[None, :] <= query_pos[:, None]) & (
                query_pos[:, None] <= key_end[None, :]
            )
            scores = (
                jnp.einsum("tkgd,skd->kgts", queries, key_rows, preferred_element_type=jnp.float32)
                * score_scale
            )
            return (row_start, key_rows, value_rows, visible, scores)

        def max_step(listed_slot, loop_carry):
            row_max, row_total = loop_carry
            _, _, _, visible, scores = block_terms(listed_slot)
            masked = jnp.where(visible, scores, masked_value)
            new_max = jnp.maximum(row_max, jnp.max(masked, axis=-1))
            row_total = row_total * jnp.exp(row_max - new_max) + jnp.sum(
                jnp.where(visible, jnp.exp(masked - new_max[..., None]), 0.0), axis=-1
            )
            return (new_max, row_total)

        row_max, row_total = lax.fori_loop(
            0,
            listed_count,
            max_step,
            (jnp.full(stats_shape, masked_value, jnp.float32), jnp.zeros(stats_shape, jnp.float32)),
        )
        log_total = row_max + jnp.log(row_total)

        def value_step(listed_slot, attended_sum, log_total=log_total):
            _, _, value_rows, visible, scores = block_terms(listed_slot)
            probability_low = jnp.where(
                visible, jnp.exp(scores - log_total[..., None]), 0.0
            ).astype(jnp.bfloat16)
            return attended_sum + jnp.einsum(
                "kgts,skd->tkgd", probability_low, value_rows, preferred_element_type=jnp.float32
            )

        attended = lax.fori_loop(
            0,
            listed_count,
            value_step,
            jnp.zeros((BLK, kv_local, group_size, head_width), jnp.float32),
        ).astype(jnp.bfloat16)
        inner_product = jnp.transpose(
            jnp.sum(grad_rows.astype(jnp.float32) * widen(attended), axis=-1), (1, 2, 0)
        )

        def grad_step(
            listed_slot,
            loop_carry,
            log_total=log_total,
            inner_product=inner_product,
            queries=queries,
            grad_rows=grad_rows,
        ):
            query_sum, key_sum, value_sum = loop_carry
            row_start, key_rows, value_rows, visible, scores = block_terms(listed_slot)
            probability = jnp.where(visible, jnp.exp(scores - log_total[..., None]), 0.0)
            probability_low = probability.astype(jnp.bfloat16)
            dprob = jnp.einsum(
                "tkgd,skd->kgts", grad_rows, value_rows, preferred_element_type=jnp.float32
            )
            dscore_low = (probability * (dprob - inner_product[..., None]) * score_scale).astype(
                jnp.bfloat16
            )
            query_sum = query_sum + jnp.einsum(
                "kgts,skd->tkgd", dscore_low, key_rows, preferred_element_type=jnp.float32
            )
            key_part = jnp.einsum(
                "kgts,tkgd->skd", dscore_low, queries, preferred_element_type=jnp.float32
            )
            value_part = jnp.einsum(
                "kgts,tkgd->skd", probability_low, grad_rows, preferred_element_type=jnp.float32
            )
            key_sum = lax.dynamic_update_slice_in_dim(
                key_sum,
                lax.dynamic_slice_in_dim(key_sum, row_start, BLK, 0) + key_part,
                row_start,
                0,
            )
            value_sum = lax.dynamic_update_slice_in_dim(
                value_sum,
                lax.dynamic_slice_in_dim(value_sum, row_start, BLK, 0) + value_part,
                row_start,
                0,
            )
            return (query_sum, key_sum, value_sum)

        query_start = jnp.zeros((BLK, kv_local, group_size, head_width), jnp.float32)
        query_grad, key_grad, value_grad = lax.fori_loop(
            0, listed_count, grad_step, (query_start, key_grad, value_grad)
        )
        out_blocks.append(attended.reshape(BLK, kv_local * group_size, head_width))
        query_blocks.append(
            query_grad.astype(jnp.bfloat16).reshape(BLK, kv_local * group_size, head_width)
        )
    grad_window = jnp.stack([key_grad, value_grad])

    def window_part(offset):
        return lax.slice_in_dim(
            grad_window, (WIN - offset) * tok_dev, (WIN - offset + 1) * tok_dev, axis=1
        )

    summed = window_part(WIN)
    for offset in range(WIN - 1, -1, -1):
        summed = window_part(offset) + from_behind(summed.astype(jnp.bfloat16), "seq", -1).astype(
            summed.dtype
        )
    attended_all = jnp.concatenate(out_blocks, axis=0)
    dq_rot = jnp.concatenate(query_blocks, axis=0)
    dk_rot = summed[0].astype(jnp.bfloat16)
    dv_local = summed[1].astype(jnp.bfloat16)
    attn_out, dq_tokens, dk_tokens, dv_grad = (
        lax.all_to_all(attended_all, "kv", split_axis=0, concat_axis=1, tiled=True),
        lax.all_to_all(dq_rot, "kv", split_axis=0, concat_axis=1, tiled=True),
        lax.all_to_all(dk_rot, "kv", split_axis=0, concat_axis=1, tiled=True),
        lax.all_to_all(dv_local, "kv", split_axis=0, concat_axis=1, tiled=True),
    )
    dq_grad = rope_back(widen(dq_tokens), cosine, sine).astype(jnp.bfloat16)
    dk_grad = rope_back(widen(dk_tokens), cosine, sine).astype(jnp.bfloat16)
    return (attn_out, dq_grad, dk_grad, dv_grad)


def solution(mesh):
    in_specs = (
        P(("seq", "kv"), None, None),
        P(("seq", "kv"), None, None),
        P(("seq", "kv"), None, None),
        P(("seq", "kv"), None, None),
        P(("seq", "kv")),
        P(),
        P("seq", None),
    )
    out_specs = (
        P(("seq", "kv"), None, None),
        P(("seq", "kv"), None, None),
        P(("seq", "kv"), None, None),
        P(("seq", "kv"), None, None),
    )
    return jax.shard_map(body, mesh=mesh, in_specs=in_specs, out_specs=out_specs, check_vma=False)
```

profile of v0, /device:TPU:8, one launch (start us, length us, event | category | flops | bytes accessed | tf_op | source)
XLA Modules:
  0.0 400.9 jit_solution(17787525584119715119)
XLA Ops:
  4.1 4.3 %all-to-all-start = ((bf16[32,8,128]{2,0,1:T(8,128)(2,1)}), bf16[32,8,128]{2,0,1:T(8,128)(2,1)S(1)}, u32[]{:S(2)}, u32[]{:S(2)}) async-start(bf16[32,8,128]{2,0,1:T(8,128)(2,1)} %fusion.167), calls=%async_computation | async-start | bytes 131072 | tf_op jit(solution)/shard_map/all_to_all | solution.py:58
  10.4 3.7 all-to-all-done
  19.0 3.9 all-to-all-done.1
  23.0 3.5 all-to-all-start.2
  26.5 13.2 %collective-permute-start = (bf16[2,256,1,128]{3,1,2,0:T(8,128)(2,1)S(1)}, bf16[2,256,1,128]{3,1,2,0:T(8,128)(2,1)S(1)}, u32[]{:S(2)}, u32[]{:S(2)}) collective-permute-start(bf16[2,256,1,128]{3,1,2,0:T(8,128)(2,1)S(1)} %pad_maximum_fusion.3), channel_id=1, source_target_pairs={{0,56},{8,64},{16,72},{24,80},{32,88},{40,96},{48,104},{56,112},{6... | collective-permute-start | bytes 393224 | tf_op jit(solution)/shard_map/ppermute | solution.py:19
  39.7 7.3 %collective-permute-start.1 = (bf16[2,256,1,128]{3,1,2,0:T(8,128)(2,1)S(1)}, bf16[2,256,1,128]{3,1,2,0:T(8,128)(2,1)S(1)}, u32[]{:S(2)}, u32[]{:S(2)}) collective-permute-start(bf16[2,256,1,128]{3,1,2,0:T(8,128)(2,1)S(1)} %pad_maximum_fusion.3), channel_id=1, source_target_pairs={{0,48},{8,56},{16,64},{24,72},{32,80},{40,88},{48,96},{56,104},{64... | collective-permute-start | bytes 393224 | tf_op jit(solution)/shard_map/ppermute | solution.py:19
  50.7 7.5 %collective-permute-start.3 = (bf16[2,256,1,128]{3,1,2,0:T(8,128)(2,1)S(1)}, bf16[2,256,1,128]{3,1,2,0:T(8,128)(2,1)S(1)}, u32[]{:S(2)}, u32[]{:S(2)}) collective-permute-start(bf16[2,256,1,128]{3,1,2,0:T(8,128)(2,1)S(1)} %pad_maximum_fusion.3), channel_id=1, source_target_pairs={{0,32},{8,40},{16,48},{24,56},{32,64},{40,72},{48,80},{56,88},{64,... | collective-permute-start | bytes 393224 | tf_op jit(solution)/shard_map/ppermute | solution.py:19
  58.2 6.8 %collective-permute-start.4 = (bf16[2,256,1,128]{3,1,2,0:T(8,128)(2,1)S(1)}, bf16[2,256,1,128]{3,1,2,0:T(8,128)(2,1)S(1)}, u32[]{:S(2)}, u32[]{:S(2)}) collective-permute-start(bf16[2,256,1,128]{3,1,2,0:T(8,128)(2,1)S(1)} %pad_maximum_fusion.3), channel_id=1, source_target_pairs={{0,24},{8,32},{16,40},{24,48},{32,56},{40,64},{48,72},{56,80},{64,... | collective-permute-start | bytes 393224 | tf_op jit(solution)/shard_map/ppermute | solution.py:19
  65.0 4.7 %collective-permute-start.5 = (bf16[2,256,1,128]{3,1,2,0:T(8,128)(2,1)S(1)}, bf16[2,256,1,128]{3,1,2,0:T(8,128)(2,1)S(1)}, u32[]{:S(2)}, u32[]{:S(2)}) collective-permute-start(bf16[2,256,1,128]{3,1,2,0:T(8,128)(2,1)S(1)} %pad_maximum_fusion.3), channel_id=1, source_target_pairs={{0,16},{8,24},{16,32},{24,40},{32,48},{40,56},{48,64},{56,72},{64,... | collective-permute-start | bytes 393224 | tf_op jit(solution)/shard_map/ppermute | solution.py:19
  73.1 9.5 %collective-permute-start.6 = (bf16[2,256,1,128]{3,1,2,0:T(8,128)(2,1)S(1)}, bf16[2,256,1,128]{3,1,2,0:T(8,128)(2,1)S(1)}, u32[]{:S(2)}, u32[]{:S(2)}) collective-permute-start(bf16[2,256,1,128]{3,1,2,0:T(8,128)(2,1)S(1)} %pad_maximum_fusion.3), channel_id=1, source_target_pairs={{0,8},{8,16},{16,24},{24,32},{32,40},{40,48},{48,56},{56,64},{64,7... | collective-permute-start | bytes 393224 | tf_op jit(solution)/shard_map/ppermute | solution.py:19
  82.6 14.5 %collective-permute-done.2 = bf16[2,256,1,128]{3,1,2,0:T(8,128)(2,1)S(1)} collective-permute-done((bf16[2,256,1,128]{3,1,2,0:T(8,128)(2,1)S(1)}, bf16[2,256,1,128]{3,1,2,0:T(8,128)(2,1)S(1)}, u32[]{:S(2)}, u32[]{:S(2)}) %collective-permute-start.2) | collective-permute-done | bytes 131104 | tf_op jit(solution)/shard_map/ppermute | solution.py:19
  99.4 12.9 %collective-permute-done.4 = bf16[2,256,1,128]{3,1,2,0:T(8,128)(2,1)S(1)} collective-permute-done((bf16[2,256,1,128]{3,1,2,0:T(8,128)(2,1)S(1)}, bf16[2,256,1,128]{3,1,2,0:T(8,128)(2,1)S(1)}, u32[]{:S(2)}, u32[]{:S(2)}) %collective-permute-start.4) | collective-permute-done | bytes 131104 | tf_op jit(solution)/shard_map/ppermute | solution.py:19
  112.3 4.1 %collective-permute-done.5 = bf16[2,256,1,128]{3,1,2,0:T(8,128)(2,1)S(1)} collective-permute-done((bf16[2,256,1,128]{3,1,2,0:T(8,128)(2,1)S(1)}, bf16[2,256,1,128]{3,1,2,0:T(8,128)(2,1)S(1)}, u32[]{:S(2)}, u32[]{:S(2)}) %collective-permute-start.5) | collective-permute-done | bytes 131104 | tf_op jit(solution)/shard_map/ppermute | solution.py:19
  120.0 4.5 %all-to-all-start.4 = ((bf16[32,64,128]{2,0,1:T(8,128)(2,1)}), bf16[32,64,128]{2,0,1:T(8,128)(2,1)S(1)}, u32[]{:S(2)}, u32[]{:S(2)}) async-start(bf16[32,64,128]{2,0,1:T(8,128)(2,1)} %copy.137), calls=%async_computation.4 | async-start | bytes 1048576 | tf_op jit(solution)/shard_map/all_to_all | solution.py:57
  124.6 16.0 %while.78 = (s32[]{:T(128)}, f32[1,8,128]{2,1,0:T(8,128)S(1)}, f32[1,8,128]{2,1,0:T(8,128)S(1)}, s32[]{:T(128)}, s32[6]{0:T(128)S(1)}, /*index=5*/s32[16384]{0:T...) while((s32[]{:T(128)}, f32[1,8,128]{2,1,0:T(8,128)S(1)}, ...), condition=%wide.region_4.5_spmd.clone, body=%wide.region_1.4_spmd.clone.sunk | while | flops 34392332 | bytes 1449787 | solution.py:118
  140.6 16.2 %while.79 = (s32[]{:T(128)}, f32[128,1,8,128]{0,3,2,1:T(8,128)S(1)}, s32[]{:T(128)}, s32[6]{0:T(128)S(1)}, s32[]{:T(128)}, /*index=5*/bf16[2048,1,128]{0,2,1:T(8...) while((s32[]{:T(128)}, ...), condition=%wide.region_6.7_spmd.clone, body=%wide.region_5.6_spmd.clone.sunk | while | flops 67813648 | bytes 1418047 | solution.py:135
  159.4 28.5 %while.82 = (s32[]{:T(128)}, f32[128,1,8,128]{0,3,2,1:T(8,128)S(1)}, f32[2048,1,128]{2,0,1:T(8,128)S(1)}, f32[2048,1,128]{2,0,1:T(8,128)S(1)}, s32[]{:T(128)}, /...) while((s32[]{:T(128)}, ...), condition=%wide.region_16.17_spmd.clone, body=%wide.region_15.16_spmd.clone.sunk | while | flops 169034000 | bytes 4861811 | solution.py:187
  188.7 9.6 %while.80 = (s32[]{:T(128)}, f32[1,8,128]{2,1,0:T(8,128)S(1)}, f32[1,8,128]{2,1,0:T(8,128)S(1)}, s32[]{:T(128)}, s32[6]{0:T(128)S(1)}, /*index=5*/s32[16384]{0:T...) while((s32[]{:T(128)}, f32[1,8,128]{2,1,0:T(8,128)S(1)}, ...), condition=%wide.region_11.12_spmd.clone, body=%wide.region_8.11_spmd.clone.sunk | while | flops 34392332 | bytes 1449787 | solution.py:118
  198.4 9.7 %while.81 = (s32[]{:T(128)}, f32[128,1,8,128]{0,3,2,1:T(8,128)S(1)}, s32[]{:T(128)}, s32[6]{0:T(128)S(1)}, s32[]{:T(128)}, /*index=5*/bf16[2048,1,128]{0,2,1:T(8...) while((s32[]{:T(128)}, ...), condition=%wide.region_13.0_spmd.clone, body=%wide.region_12.0_spmd.clone.sunk | while | flops 67813648 | bytes 1418047 | solution.py:135
  210.7 14.3 %while.83 = (s32[]{:T(128)}, f32[128,1,8,128]{0,3,2,1:T(8,128)S(1)}, f32[2048,1,128]{2,0,1:T(8,128)S(1)}, f32[2048,1,128]{2,0,1:T(8,128)S(1)}, s32[]{:T(128)}, /...) while((s32[]{:T(128)}, ...), condition=%wide.region_19.20_spmd.clone, body=%wide.region_18.19_spmd.clone.sunk | while | flops 169034000 | bytes 4861811 | solution.py:187
  227.0 5.9 %collective-permute-done.7 = bf16[2,256,1,128]{3,1,2,0:T(8,128)(2,1)S(1)} collective-permute-done((bf16[2,256,1,128]{3,1,2,0:T(8,128)(2,1)S(1)}, bf16[2,256,1,128]{3,1,2,0:T(8,128)(2,1)S(1)}, u32[]{:S(2)}, u32[]{:S(2)}) %collective-permute-start.7) | collective-permute-done | bytes 131104 | tf_op jit(solution)/shard_map/ppermute | solution.py:19
  232.9 4.3 %collective-permute-start.8 = (bf16[2,256,1,128]{3,1,2,0:T(8,128)(2,1)S(1)}, bf16[2,256,1,128]{3,1,2,0:T(8,128)(2,1)S(1)}, u32[]{:S(2)}, u32[]{:S(2)}) collective-permute-start(bf16[2,256,1,128]{3,1,2,0:T(8,128)(2,1)S(1)} %fusion.146), channel_id=1, source_target_pairs={{8,0},{16,8},{24,16},{32,24},{40,32},{48,40},{56,48},{64,56},{72,6... | collective-permute-start | bytes 393224 | tf_op jit(solution)/shard_map/ppermute | solution.py:19
  240.1 77.3 %collective-permute-start.9 = (bf16[2,256,1,128]{3,1,2,0:T(8,128)(2,1)S(1)}, bf16[2,256,1,128]{3,1,2,0:T(8,128)(2,1)S(1)}, u32[]{:S(2)}, u32[]{:S(2)}) collective-permute-start(bf16[2,256,1,128]{3,1,2,0:T(8,128)(2,1)S(1)} %fusion.164), channel_id=1, source_target_pairs={{8,0},{16,8},{24,16},{32,24},{40,32},{48,40},{56,48},{64,56},{72,6... | collective-permute-start | bytes 393224 | tf_op jit(solution)/shard_map/ppermute | solution.py:19
  320.6 6.5 %collective-permute-start.10 = (bf16[2,256,1,128]{3,1,2,0:T(8,128)(2,1)}, bf16[2,256,1,128]{3,1,2,0:T(8,128)(2,1)}, u32[]{:S(2)}, u32[]{:S(2)}) collective-permute-start(bf16[2,256,1,128]{3,1,2,0:T(8,128)(2,1)} %fusion.161), channel_id=1, source_target_pairs={{8,0},{16,8},{24,16},{32,24},{40,32},{48,40},{56,48},{64,56},{72,6... | collective-permute-start | bytes 393224 | tf_op jit(solution)/shard_map/ppermute | solution.py:19
  330.8 6.5 %collective-permute-start.11 = (bf16[2,256,1,128]{3,1,2,0:T(8,128)(2,1)S(1)}, bf16[2,256,1,128]{3,1,2,0:T(8,128)(2,1)S(1)}, u32[]{:S(2)}, u32[]{:S(2)}) collective-permute-start(bf16[2,256,1,128]{3,1,2,0:T(8,128)(2,1)S(1)} %fusion.158), channel_id=1, source_target_pairs={{8,0},{16,8},{24,16},{32,24},{40,32},{48,40},{56,48},{64,56},{72,6... | collective-permute-start | bytes 393224 | tf_op jit(solution)/shard_map/ppermute | solution.py:19
  338.1 4.3 %all-to-all-start.5 = ((bf16[256,8,128]{2,1,0:T(8,128)(2,1)}), bf16[256,8,128]{2,1,0:T(8,128)(2,1)S(1)}, u32[]{:S(2)}, u32[]{:S(2)}) async-start(bf16[256,8,128]{2,1,0:T(8,128)(2,1)} %pad_maximum_fusion.1), calls=%async_computation.5 | async-start | bytes 1048576 | tf_op jit(solution)/shard_map/all_to_all | solution.py:212
  342.5 12.7 %collective-permute-done.11 = bf16[2,256,1,128]{3,1,2,0:T(8,128)(2,1)S(1)} collective-permute-done((bf16[2,256,1,128]{3,1,2,0:T(8,128)(2,1)S(1)}, bf16[2,256,1,128]{3,1,2,0:T(8,128)(2,1)S(1)}, u32[]{:S(2)}, u32[]{:S(2)}) %collective-permute-start.11) | collective-permute-done | bytes 131104 | tf_op jit(solution)/shard_map/ppermute | solution.py:19
  358.0 4.1 %all-to-all-start.3 = ((bf16[256,8,128]{2,1,0:T(8,128)(2,1)}), bf16[256,8,128]{2,1,0:T(8,128)(2,1)S(1)}, u32[]{:S(2)}, u32[]{:S(2)}) async-start(bf16[256,8,128]{2,1,0:T(8,128)(2,1)} %pad_maximum_fusion), calls=%async_computation.3 | async-start | bytes 1048576 | tf_op jit(solution)/shard_map/all_to_all | solution.py:211
  368.6 9.8 %collective-permute-done.13 = bf16[2,256,1,128]{3,1,2,0:T(8,128)(2,1)S(1)} collective-permute-done((bf16[2,256,1,128]{3,1,2,0:T(8,128)(2,1)S(1)}, bf16[2,256,1,128]{3,1,2,0:T(8,128)(2,1)S(1)}, u32[]{:S(2)}, u32[]{:S(2)}) %collective-permute-start.13) | collective-permute-done | bytes 131104 | tf_op jit(solution)/shard_map/ppermute | solution.py:19
  380.2 4.5 %all-to-all-start.6 = ((bf16[8,2,2048]{2,1,0:T(2,128)(2,1)}), bf16[8,2,2048]{2,1,0:T(2,128)(2,1)S(1)}, u32[]{:S(2)}, u32[]{:S(2)}) async-start(bf16[8,2,2048]{2,1,0:T(2,128)(2,1)} %reshape.317), calls=%async_computation.6 | async-start | bytes 131072 | tf_op jit(solution)/shard_map/all_to_all | solution.py:213
  390.3 4.2 %all-to-all-start.7 = ((bf16[8,2,2048]{2,1,0:T(2,128)(2,1)}), bf16[8,2,2048]{2,1,0:T(2,128)(2,1)S(1)}, u32[]{:S(2)}, u32[]{:S(2)}) async-start(bf16[8,2,2048]{2,1,0:T(2,128)(2,1)} %reshape.319), calls=%async_computation.7 | async-start | bytes 131072 | tf_op jit(solution)/shard_map/all_to_all | solution.py:214
  395.5 4.6 %all-to-all-done.7 = bf16[8,2,2048]{2,1,0:T(2,128)(2,1)S(1)} async-done(((bf16[8,2,2048]{2,1,0:T(2,128)(2,1)}), bf16[8,2,2048]{2,1,0:T(2,128)(2,1)S(1)}, u32[]{:S(2)}, u32[]{:S(2)}) %all-to-all-start.7) | async-done | bytes 65568 | tf_op jit(solution)/shard_map/all_to_all | solution.py:214
  (270 shorter events, 115.6 us)
Async XLA Ops:
  0.6 7.8 %copy-start.2 = (bf16[32,64,128]{2,1,0:T(8,128)(2,1)S(1)}, bf16[32,64,128]{2,1,0:T(8,128)(2,1)}, u32[]{:S(2)}) copy-start(bf16[32,64,128]{2,1,0:T(8,128)(2,1)} %param.19) | copy-start | bytes 1572868
  4.1 9.9 %all-to-all-start = ((bf16[32,8,128]{2,0,1:T(8,128)(2,1)}), bf16[32,8,128]{2,0,1:T(8,128)(2,1)S(1)}, u32[]{:S(2)}, u32[]{:S(2)}) async-start(bf16[32,8,128]{2,0,1:T(8,128)(2,1)} %fusion.167), calls=%async_computation | async-start | bytes 131072 | tf_op jit(solution)/shard_map/all_to_all | solution.py:58
  14.1 8.9 %all-to-all-start.1 = ((bf16[32,8,128]{2,0,1:T(8,128)(2,1)}), bf16[32,8,128]{2,0,1:T(8,128)(2,1)S(1)}, u32[]{:S(2)}, u32[]{:S(2)}) async-start(bf16[32,8,128]{2,0,1:T(8,128)(2,1)} %copy.128), calls=%async_computation.1 | async-start | bytes 131072 | tf_op jit(solution)/shard_map/all_to_all | solution.py:59
  17.9 21.8 %copy-start.13 = (s32[2,6]{1,0:T(2,128)S(1)}, s32[2,6]{1,0:T(2,128)}, u32[]{:S(2)}) copy-start(s32[2,6]{1,0:T(2,128)} %param.25) | copy-start | bytes 148
  17.9 29.7 %copy-start.11 = (bf16[32,64,128]{2,1,0:T(8,128)(2,1)S(1)}, bf16[32,64,128]{2,1,0:T(8,128)(2,1)}, u32[]{:S(2)}) copy-start(bf16[32,64,128]{2,1,0:T(8,128)(2,1)} %param.22) | copy-start | bytes 1572868
  23.0 96.5 %all-to-all-start.2 = ((bf16[32,64,128]{2,0,1:T(8,128)(2,1)}), bf16[32,64,128]{2,0,1:T(8,128)(2,1)S(1)}, u32[]{:S(2)}, u32[]{:S(2)}) async-start(bf16[32,64,128]{2,0,1:T(8,128)(2,1)} %copy.129), calls=%async_computation.2 | async-start | bytes 1048576 | tf_op jit(solution)/shard_map/all_to_all | solution.py:56
  26.5 38.5 %collective-permute-start = (bf16[2,256,1,128]{3,1,2,0:T(8,128)(2,1)S(1)}, bf16[2,256,1,128]{3,1,2,0:T(8,128)(2,1)S(1)}, u32[]{:S(2)}, u32[]{:S(2)}) collective-permute-start(bf16[2,256,1,128]{3,1,2,0:T(8,128)(2,1)S(1)} %pad_maximum_fusion.3), channel_id=1, source_target_pairs={{0,56},{8,64},{16,72},{24,80},{32,88},{40,96},{48,104},{56,112},{6... | collective-permute-start | bytes 393224 | tf_op jit(solution)/shard_map/ppermute | solution.py:19
  39.7 33.4 %collective-permute-start.1 = (bf16[2,256,1,128]{3,1,2,0:T(8,128)(2,1)S(1)}, bf16[2,256,1,128]{3,1,2,0:T(8,128)(2,1)S(1)}, u32[]{:S(2)}, u32[]{:S(2)}) collective-permute-start(bf16[2,256,1,128]{3,1,2,0:T(8,128)(2,1)S(1)} %pad_maximum_fusion.3), channel_id=1, source_target_pairs={{0,48},{8,56},{16,64},{24,72},{32,80},{40,88},{48,96},{56,104},{64... | collective-permute-start | bytes 393224 | tf_op jit(solution)/shard_map/ppermute | solution.py:19
  48.8 48.3 %collective-permute-start.2 = (bf16[2,256,1,128]{3,1,2,0:T(8,128)(2,1)S(1)}, bf16[2,256,1,128]{3,1,2,0:T(8,128)(2,1)S(1)}, u32[]{:S(2)}, u32[]{:S(2)}) collective-permute-start(bf16[2,256,1,128]{3,1,2,0:T(8,128)(2,1)S(1)} %pad_maximum_fusion.3), channel_id=1, source_target_pairs={{0,40},{8,48},{16,56},{24,64},{32,72},{40,80},{48,88},{56,96},{64,... | collective-permute-start | bytes 393224 | tf_op jit(solution)/shard_map/ppermute | solution.py:19
  50.7 48.7 %collective-permute-start.3 = (bf16[2,256,1,128]{3,1,2,0:T(8,128)(2,1)S(1)}, bf16[2,256,1,128]{3,1,2,0:T(8,128)(2,1)S(1)}, u32[]{:S(2)}, u32[]{:S(2)}) collective-permute-start(bf16[2,256,1,128]{3,1,2,0:T(8,128)(2,1)S(1)} %pad_maximum_fusion.3), channel_id=1, source_target_pairs={{0,32},{8,40},{16,48},{24,56},{32,64},{40,72},{48,80},{56,88},{64,... | collective-permute-start | bytes 393224 | tf_op jit(solution)/shard_map/ppermute | solution.py:19
  58.2 54.1 %collective-permute-start.4 = (bf16[2,256,1,128]{3,1,2,0:T(8,128)(2,1)S(1)}, bf16[2,256,1,128]{3,1,2,0:T(8,128)(2,1)S(1)}, u32[]{:S(2)}, u32[]{:S(2)}) collective-permute-start(bf16[2,256,1,128]{3,1,2,0:T(8,128)(2,1)S(1)} %pad_maximum_fusion.3), channel_id=1, source_target_pairs={{0,24},{8,32},{16,40},{24,48},{32,56},{40,64},{48,72},{56,80},{64,... | collective-permute-start | bytes 393224 | tf_op jit(solution)/shard_map/ppermute | solution.py:19
  65.0 51.3 %collective-permute-start.5 = (bf16[2,256,1,128]{3,1,2,0:T(8,128)(2,1)S(1)}, bf16[2,256,1,128]{3,1,2,0:T(8,128)(2,1)S(1)}, u32[]{:S(2)}, u32[]{:S(2)}) collective-permute-start(bf16[2,256,1,128]{3,1,2,0:T(8,128)(2,1)S(1)} %pad_maximum_fusion.3), channel_id=1, source_target_pairs={{0,16},{8,24},{16,32},{24,40},{32,48},{40,56},{48,64},{56,72},{64,... | collective-permute-start | bytes 393224 | tf_op jit(solution)/shard_map/ppermute | solution.py:19
  73.1 46.0 %collective-permute-start.6 = (bf16[2,256,1,128]{3,1,2,0:T(8,128)(2,1)S(1)}, bf16[2,256,1,128]{3,1,2,0:T(8,128)(2,1)S(1)}, u32[]{:S(2)}, u32[]{:S(2)}) collective-permute-start(bf16[2,256,1,128]{3,1,2,0:T(8,128)(2,1)S(1)} %pad_maximum_fusion.3), channel_id=1, source_target_pairs={{0,8},{8,16},{16,24},{24,32},{32,40},{40,48},{48,56},{56,64},{64,7... | collective-permute-start | bytes 393224 | tf_op jit(solution)/shard_map/ppermute | solution.py:19
  120.0 37.9 %all-to-all-start.4 = ((bf16[32,64,128]{2,0,1:T(8,128)(2,1)}), bf16[32,64,128]{2,0,1:T(8,128)(2,1)S(1)}, u32[]{:S(2)}, u32[]{:S(2)}) async-start(bf16[32,64,128]{2,0,1:T(8,128)(2,1)} %copy.137), calls=%async_computation.4 | async-start | bytes 1048576 | tf_op jit(solution)/shard_map/all_to_all | solution.py:57
  157.6 1.2 copy-start.3
  157.9 1.0 copy-start.5
  208.4 2.4 copy-start.7
  225.1 7.8 %collective-permute-start.7 = (bf16[2,256,1,128]{3,1,2,0:T(8,128)(2,1)S(1)}, bf16[2,256,1,128]{3,1,2,0:T(8,128)(2,1)S(1)}, u32[]{:S(2)}, u32[]{:S(2)}) collective-permute-start(bf16[2,256,1,128]{3,1,2,0:T(8,128)(2,1)S(1)} %fusion.165), channel_id=1, source_target_pairs={{8,0},{16,8},{24,16},{32,24},{40,32},{48,40},{56,48},{64,56},{72,6... | collective-permute-start | bytes 393224 | tf_op jit(solution)/shard_map/ppermute | solution.py:19
  232.9 7.2 %collective-permute-start.8 = (bf16[2,256,1,128]{3,1,2,0:T(8,128)(2,1)S(1)}, bf16[2,256,1,128]{3,1,2,0:T(8,128)(2,1)S(1)}, u32[]{:S(2)}, u32[]{:S(2)}) collective-permute-start(bf16[2,256,1,128]{3,1,2,0:T(8,128)(2,1)S(1)} %fusion.146), channel_id=1, source_target_pairs={{8,0},{16,8},{24,16},{32,24},{40,32},{48,40},{56,48},{64,56},{72,6... | collective-permute-start | bytes 393224 | tf_op jit(solution)/shard_map/ppermute | solution.py:19
  240.1 87.2 %copy-start.1 = (f32[128,1,8,128]{0,3,2,1:T(8,128)S(1)}, f32[128,1,8,128]{0,3,2,1:T(8,128)}, u32[]{:S(2)}) copy-start(f32[128,1,8,128]{0,3,2,1:T(8,128)} %copy-done) | copy-start | bytes 1572868
  240.1 79.8 %collective-permute-start.9 = (bf16[2,256,1,128]{3,1,2,0:T(8,128)(2,1)S(1)}, bf16[2,256,1,128]{3,1,2,0:T(8,128)(2,1)S(1)}, u32[]{:S(2)}, u32[]{:S(2)}) collective-permute-start(bf16[2,256,1,128]{3,1,2,0:T(8,128)(2,1)S(1)} %fusion.164), channel_id=1, source_target_pairs={{8,0},{16,8},{24,16},{32,24},{40,32},{48,40},{56,48},{64,56},{72,6... | collective-permute-start | bytes 393224 | tf_op jit(solution)/shard_map/ppermute | solution.py:19
  320.6 9.3 %collective-permute-start.10 = (bf16[2,256,1,128]{3,1,2,0:T(8,128)(2,1)}, bf16[2,256,1,128]{3,1,2,0:T(8,128)(2,1)}, u32[]{:S(2)}, u32[]{:S(2)}) collective-permute-start(bf16[2,256,1,128]{3,1,2,0:T(8,128)(2,1)} %fusion.161), channel_id=1, source_target_pairs={{8,0},{16,8},{24,16},{32,24},{40,32},{48,40},{56,48},{64,56},{72,6... | collective-permute-start | bytes 393224 | tf_op jit(solution)/shard_map/ppermute | solution.py:19
  330.8 24.4 %collective-permute-start.11 = (bf16[2,256,1,128]{3,1,2,0:T(8,128)(2,1)S(1)}, bf16[2,256,1,128]{3,1,2,0:T(8,128)(2,1)S(1)}, u32[]{:S(2)}, u32[]{:S(2)}) collective-permute-start(bf16[2,256,1,128]{3,1,2,0:T(8,128)(2,1)S(1)} %fusion.158), channel_id=1, source_target_pairs={{8,0},{16,8},{24,16},{32,24},{40,32},{48,40},{56,48},{64,56},{72,6... | collective-permute-start | bytes 393224 | tf_op jit(solution)/shard_map/ppermute | solution.py:19
  338.1 19.9 %all-to-all-start.5 = ((bf16[256,8,128]{2,1,0:T(8,128)(2,1)}), bf16[256,8,128]{2,1,0:T(8,128)(2,1)S(1)}, u32[]{:S(2)}, u32[]{:S(2)}) async-start(bf16[256,8,128]{2,1,0:T(8,128)(2,1)} %pad_maximum_fusion.1), calls=%async_computation.5 | async-start | bytes 1048576 | tf_op jit(solution)/shard_map/all_to_all | solution.py:212
  342.5 14.7 %copy-start.6 = (bf16[128,1,8,128]{3,2,0,1:T(8,128)(2,1)S(1)}, bf16[128,1,8,128]{3,2,0,1:T(8,128)(2,1)}, u32[]{:S(2)}) copy-start(bf16[128,1,8,128]{3,2,0,1:T(8,128)(2,1)} %copy-done.5) | copy-start | bytes 786436
  342.5 14.7 %copy-start.8 = (bf16[128,1,8,128]{3,2,0,1:T(8,128)(2,1)S(1)}, bf16[128,1,8,128]{3,2,0,1:T(8,128)(2,1)}, u32[]{:S(2)}) copy-start(bf16[128,1,8,128]{3,2,0,1:T(8,128)(2,1)} %copy-done.7) | copy-start | bytes 786436
  355.2 8.2 %collective-permute-start.12 = (bf16[2,256,1,128]{3,1,2,0:T(8,128)(2,1)S(1)}, bf16[2,256,1,128]{3,1,2,0:T(8,128)(2,1)S(1)}, u32[]{:S(2)}, u32[]{:S(2)}) collective-permute-start(bf16[2,256,1,128]{3,1,2,0:T(8,128)(2,1)S(1)} %fusion.155), channel_id=1, source_target_pairs={{8,0},{16,8},{24,16},{32,24},{40,32},{48,40},{56,48},{64,56},{72,6... | collective-permute-start | bytes 393224 | tf_op jit(solution)/shard_map/ppermute | solution.py:19
  358.0 4.1 %copy-start.9 = (bf16[256,8,128]{2,1,0:T(8,128)(2,1)}, bf16[256,8,128]{2,1,0:T(8,128)(2,1)S(1)}, u32[]{:S(2)}) copy-start(bf16[256,8,128]{2,1,0:T(8,128)(2,1)S(1)} %all-to-all-done.5) | copy-start | bytes 1572868
  358.0 22.2 %all-to-all-start.3 = ((bf16[256,8,128]{2,1,0:T(8,128)(2,1)}), bf16[256,8,128]{2,1,0:T(8,128)(2,1)S(1)}, u32[]{:S(2)}, u32[]{:S(2)}) async-start(bf16[256,8,128]{2,1,0:T(8,128)(2,1)} %pad_maximum_fusion), calls=%async_computation.3 | async-start | bytes 1048576 | tf_op jit(solution)/shard_map/all_to_all | solution.py:211
  363.5 14.9 %collective-permute-start.13 = (bf16[2,256,1,128]{3,1,2,0:T(8,128)(2,1)S(1)}, bf16[2,256,1,128]{3,1,2,0:T(8,128)(2,1)S(1)}, u32[]{:S(2)}, u32[]{:S(2)}) collective-permute-start(bf16[2,256,1,128]{3,1,2,0:T(8,128)(2,1)S(1)} %fusion.152), channel_id=1, source_target_pairs={{8,0},{16,8},{24,16},{32,24},{40,32},{48,40},{56,48},{64,56},{72,6... | collective-permute-start | bytes 393224 | tf_op jit(solution)/shard_map/ppermute | solution.py:19
  380.2 10.1 %all-to-all-start.6 = ((bf16[8,2,2048]{2,1,0:T(2,128)(2,1)}), bf16[8,2,2048]{2,1,0:T(2,128)(2,1)S(1)}, u32[]{:S(2)}, u32[]{:S(2)}) async-start(bf16[8,2,2048]{2,1,0:T(2,128)(2,1)} %reshape.317), calls=%async_computation.6 | async-start | bytes 131072 | tf_op jit(solution)/shard_map/all_to_all | solution.py:213
  390.3 9.8 %all-to-all-start.7 = ((bf16[8,2,2048]{2,1,0:T(2,128)(2,1)}), bf16[8,2,2048]{2,1,0:T(2,128)(2,1)S(1)}, u32[]{:S(2)}, u32[]{:S(2)}) async-start(bf16[8,2,2048]{2,1,0:T(2,128)(2,1)} %reshape.319), calls=%async_computation.7 | async-start | bytes 131072 | tf_op jit(solution)/shard_map/all_to_all | solution.py:214
  (4 other events, 3.2 us)
where the time goes:
time: 403 us; the launch traced here: 401 us
  starting transfers between devices  185 us (46%)
  waiting for transfers between devices  88.7 us (22%)
  local copies, waits for them, and re-layouts  40.9 us (10%)
  loops' own time  39.1 us (10%)
  matrix products  28 us (7%)
  other arithmetic  18.2 us (5%)
    ppermute x14, starting transfers between devices, from_behind(): lax.ppermute(value, axis, [(source, source + steps) for source in range(i...  152 us
    ppermute x14, waiting for transfers between devices, from_behind(): lax.ppermute(value, axis, [(source, source + steps) for source in range(i...  75.9 us
    dynamic_slice x18, local copies, waits for them, and re-layouts, block_terms(): key_end = lax.dynamic_slice_in_dim(subtree_end, ancestor * BLK, BLK, 0)  13.8 us
    another operation x2, loops' own time, body(): lax.fori_loop(0, listed_count, max_step, (jnp.full(stats_shape, masked_va...  13.2 us
    another operation x2, loops' own time, body(): lax.fori_loop(0, listed_count, value_step, jnp.zeros((BLK, kv_local, grou...  13 us
    another operation x2, loops' own time, body(): lax.fori_loop(0, listed_count, grad_step, (query_start, key_grad, value_g...  13 us
    dynamic_slice x18, local copies, waits for them, and re-layouts, block_terms(): ancestor = listed[listed_slot]  10.8 us
    dot_general x12, matrix products, block_terms(): jnp.einsum('tkgd,skd->kgts', queries, key_rows, preferred_element_type=jn...  9.08 us
  transfers between devices with their start and end apart: 22, of which 16 were waited for; matrix products, arithmetic and copies ran while one was open for 8% of the time, Pallas kernels for 0%

commit v1 on v0

v1 whole, which is shorter than its diff:
```python
import functools
import math

import jax
import jax.numpy as jnp
from jax import lax
from jax.experimental import pallas as pl
from jax.experimental.pallas import tpu as pltpu
from jax.sharding import PartitionSpec as P

MESH = pl.DeviceIdType.MESH
BF16, F32 = jnp.bfloat16, jnp.float32
BLK = 128
ANC = 6
WIN = 7
KV = 8
GRP = 8
TOK = 32
DH = 128
ROWS = TOK * GRP
KEYS = ANC * BLK
ROPE_BASE = 500000.0
HIDDEN = -1e30
SCALE = 1.0 / math.sqrt(DH)
LOG2E = 1.4426950408889634
NT = (((1,), (1,)), ((), ()))
NN = (((1,), (0,)), ((), ()))


def dot(a, b, dims=NN):
    return lax.dot_general(a, b, dims, preferred_element_type=F32)


def kernel(
    lines,
    q_ref, k_ref, v_ref, g_ref, cos_ref, sin_ref, anc_ref, end_ref,
    o_out, dq_out, dk_out, dv_out,
    stage, ksend, vsend, qsend, gsend, qbuf, gbuf, kwin, vwin,
    kb, vb, kbt, vbt, bias, prob, plow, dka, dva,
    osend, dqsend, orecv, dqrecv, tmp, gout, gin, dksend, dvsend, dkrecv, dvrecv,
    in_s, in_r, win_s, win_r, grad_s, grad_r, out_s, out_r,
):
    s = lax.axis_index("seq")
    j = lax.axis_index("kv")
    left, right = s - 1, s + 1

    barrier = pltpu.get_barrier_semaphore()
    for p in range(1, KV):
        peer = lax.rem(j + p, KV)
        pl.semaphore_signal(barrier, inc=1, device_id=(s, peer), device_id_type=MESH)

    @pl.when(s > 0)
    def _():
        pl.semaphore_signal(barrier, inc=1, device_id=(left, j), device_id_type=MESH)

    @pl.when(s < lines - 1)
    def _():
        pl.semaphore_signal(barrier, inc=1, device_id=(right, j), device_id_type=MESH)

    cosine = cos_ref[...][:, None, :]
    sine = sin_ref[...][:, None, :]

    def rope(x):
        return x * cosine + pltpu.roll(x, DH // 2, 2) * sine

    def rope_back(x):
        return x * cosine - pltpu.roll(x, DH // 2, 2) * sine

    stage[...] = rope(k_ref[...].astype(F32)).reshape(ROWS, DH)
    for h in range(KV):
        ksend[h] = stage[pl.ds(h, TOK, stride=KV), :].astype(BF16)
    stage[...] = v_ref[...].astype(F32).reshape(ROWS, DH)
    for h in range(KV):
        vsend[h] = stage[pl.ds(h, TOK, stride=KV), :].astype(BF16)

    pl.semaphore_wait(
        barrier, KV - 1 + (s > 0).astype(jnp.int32) + (s < lines - 1).astype(jnp.int32)
    )

    def line_copy(kind, src, dst, peer, slot, sems):
        return pltpu.make_async_remote_copy(
            src_ref=src, dst_ref=dst, send_sem=sems[0].at[kind, peer],
            recv_sem=sems[1].at[kind, slot], device_id=(s, peer), device_id_type=MESH,
        )

    def own_rows(win):
        return win.at[j // 4, pl.ds(pl.multiple_of(lax.rem(j, 4) * TOK, TOK), TOK)]

    sends = ((ksend, kwin), (vsend, vwin))
    for kind, (src, win) in enumerate(sends):
        for p in range(1, KV):
            peer = lax.rem(j + p, KV)
            line_copy(kind, src.at[peer], own_rows(win), peer, j, (in_s, in_r)).start()
    kwin[j // 4, pl.ds(pl.multiple_of(lax.rem(j, 4) * TOK, TOK), TOK), :] = ksend[j]
    vwin[j // 4, pl.ds(pl.multiple_of(lax.rem(j, 4) * TOK, TOK), TOK), :] = vsend[j]

    for pair in range(KV // 2):
        x = q_ref[:, pair * 16:(pair + 1) * 16, :].astype(F32).reshape(TOK, 2, GRP, DH)
        y = g_ref[:, pair * 16:(pair + 1) * 16, :].astype(F32).reshape(TOK, 2, GRP, DH)
        for u in range(2):
            qsend[2 * pair + u] = rope(x[:, u]).reshape(ROWS, DH).astype(BF16)
            gsend[2 * pair + u] = y[:, u].reshape(ROWS, DH).astype(BF16)
    for p in range(1, KV):
        peer = lax.rem(j + p, KV)
        line_copy(2, qsend.at[peer], qbuf.at[j], peer, j, (in_s, in_r)).start()
        line_copy(3, gsend.at[peer], gbuf.at[j], peer, j, (in_s, in_r)).start()
    qbuf[j] = qsend[j]
    gbuf[j] = gsend[j]

    def arrived(kind, peer):
        pair = ((ksend.at[peer], own_rows(kwin)), (vsend.at[peer], own_rows(vwin)),
                (qsend.at[peer], qbuf.at[j]), (gsend.at[peer], gbuf.at[j]))[kind]
        line_copy(kind, pair[0], pair[1], peer, peer, (in_s, in_r)).wait_recv()

    def hop(which, d, h):
        win = (kwin, vwin)[which]
        return pltpu.make_async_remote_copy(
            src_ref=win.at[2 * (d - 1) + h], dst_ref=win.at[2 * d + h],
            send_sem=win_s.at[2 * which + h, d], recv_sem=win_r.at[2 * which + h, d],
            device_id=(right, j), device_id_type=MESH,
        )

    for which in range(2):
        for p in range(1, KV):
            arrived(which, lax.rem(j + p, KV))
    for d in range(1, WIN + 1):
        for which in range(2):
            for h in range(2):
                if d > 1:
                    @pl.when(s >= d - 1)
                    def _():
                        hop(which, d - 1, h).wait_recv()

                @pl.when((s >= d - 1) & (s < lines - 1))
                def _():
                    hop(which, d, h).start()
        if d == 1:
            def mask_step(u, carry):
                b = u // ANC
                slot = lax.rem(u, ANC)
                a = anc_ref[b, slot]
                row = end_ref[pl.ds(jnp.maximum(a, 0), 1), :].astype(F32)
                last = jnp.broadcast_to(row, (BLK, BLK)).T
                last = jnp.where(a >= 0, last, -1.0)
                first = (a * BLK + lax.broadcasted_iota(jnp.int32, (BLK, BLK), 0)).astype(F32)
                lane = lax.broadcasted_iota(jnp.int32, (BLK, BLK), 1) // GRP
                for c in range(4):
                    for half in range(2):
                        query = ((2 * s + b) * BLK + c * TOK + half * (TOK // 2) + lane).astype(F32)
                        seen = (query >= first) & (query <= last)
                        bias[4 * b + c, pl.ds(pl.multiple_of(slot * BLK, BLK), BLK),
                             half * BLK:(half + 1) * BLK] = jnp.where(seen, 0.0, HIDDEN)
                return carry

            lax.fori_loop(0, 2 * ANC, mask_step, 0)

    for which in range(2):
        for h in range(2):
            @pl.when(s >= WIN)
            def _():
                hop(which, WIN, h).wait_recv()

    def gather_step(u, carry):
        b = u // ANC
        slot = lax.rem(u, ANC)
        a = anc_ref[b, slot]
        index = 2 * (s - lax.shift_right_arithmetic(a, 1)) + (a & 1)
        index = jnp.where(a >= 0, jnp.clip(index, 0, 2 * WIN + 1), 0)
        rows = pl.ds(pl.multiple_of(slot * BLK, BLK), BLK)
        keys, values = kwin[index], vwin[index]
        kb[b, rows, :] = keys
        vb[b, rows, :] = values
        kbt[b, :, rows] = keys.astype(F32).T.astype(BF16)
        vbt[b, :, rows] = values.astype(F32).T.astype(BF16)
        return carry

    lax.fori_loop(0, 2 * ANC, gather_step, 0)

    for kind in (2, 3):
        for p in range(1, KV):
            arrived(kind, lax.rem(j + p, KV))

    dka[...] = jnp.zeros_like(dka)
    dva[...] = jnp.zeros_like(dva)

    def chunk(i, carry):
        b = i // 4
        queries, cotangent = qbuf[i], gbuf[i]
        scores = dot(kb[b], queries, NT) * (SCALE * LOG2E) + bias[i]
        top = jnp.max(scores, axis=0, keepdims=True)
        p = jnp.exp2(scores - top)
        p = p * (1.0 / jnp.sum(p, axis=0, keepdims=True))
        low = p.astype(BF16)
        mine = pl.ds(b * ANC, ANC)
        dva[mine] += dot(low, cotangent).reshape(ANC, BLK, DH)
        attended = dot(vbt[b], low).astype(BF16)
        osend[i] = attended.astype(F32).T.astype(BF16)
        inner = jnp.sum(cotangent.astype(F32).T * attended.astype(F32), axis=0, keepdims=True)
        dprob = dot(vb[b], cotangent, NT)
        dscore = (p * (dprob - inner) * SCALE).astype(BF16)
        dka[mine] += dot(dscore, queries).reshape(ANC, BLK, DH)
        dqsend[i] = dot(kbt[b], dscore).T.astype(BF16)

        @pl.when(i != j)
        def _():
            line_copy(0, osend.at[i], orecv.at[j], i, j, (out_s, out_r)).start()
            line_copy(1, dqsend.at[i], dqrecv.at[j], i, j, (out_s, out_r)).start()

        @pl.when(i == j)
        def _():
            orecv[j] = osend[i]
            dqrecv[j] = dqsend[i]

        return carry

    lax.fori_loop(0, KV, chunk, 0)

    def back(which, d, h):
        return pltpu.make_async_remote_copy(
            src_ref=gout.at[which, 2 * d + h], dst_ref=gin.at[which, 2 * (d - 1) + h],
            send_sem=grad_s.at[2 * which + h, d], recv_sem=grad_r.at[2 * which + h, d - 1],
            device_id=(left, j), device_id_type=MESH,
        )

    def place(b, block):
        index = 2 * ANC
        for slot in range(ANC):
            hit = (anc_ref[b, slot] == block) & (block >= 0)
            index = jnp.where(hit, b * ANC + slot, index)
        return index

    for d in range(WIN, -1, -1):
        for h in range(2):
            block = 2 * (s - d) + h
            first, second = place(0, block), place(1, block)
            for which in range(2):
                acc = (dka, dva)[which]
                tmp[which, h] = acc[first] + acc[second]
        for which in range(2):
            for h in range(2):
                if d < WIN:
                    @pl.when((s >= d) & (s < lines - 1))
                    def _():
                        back(which, d + 1, h).wait_recv()
                        tmp[which, h] = tmp[which, h] + gin[which, 2 * d + h].astype(F32)
                if d > 0:
                    @pl.when(s >= d)
                    def _():
                        gout[which, 2 * d + h] = tmp[which, h].astype(BF16)
                        back(which, d, h).start()

    for which, (dst, recv) in enumerate(((dksend, dkrecv), (dvsend, dvrecv))):
        for i in range(KV):
            dst[i] = tmp[which, i // 4, (i % 4) * TOK:(i % 4 + 1) * TOK, :].astype(BF16)
        for p in range(1, KV):
            peer = lax.rem(j + p, KV)
            line_copy(2 + which, dst.at[peer], recv.at[j], peer, j, (out_s, out_r)).start()
        recv[j] = dst[j]

    def returned(kind, peer):
        src = (osend, dqsend, dksend, dvsend)[kind]
        dst = (orecv, dqrecv, dkrecv, dvrecv)[kind]
        line_copy(kind, src.at[peer], dst.at[j], peer, peer, (out_s, out_r)).wait_recv()

    for kind in range(2):
        for p in range(1, KV):
            returned(kind, lax.rem(j + p, KV))
    for pair in range(KV // 2):
        heads = slice(pair * 16, (pair + 1) * 16)
        o = [orecv[2 * pair + u].astype(F32).reshape(TOK, GRP, DH) for u in range(2)]
        o_out[:, heads, :] = jnp.concatenate(o, axis=1).astype(BF16)
        x = [rope_back(dqrecv[2 * pair + u].astype(F32).reshape(TOK, GRP, DH)) for u in range(2)]
        dq_out[:, heads, :] = jnp.concatenate(x, axis=1).astype(BF16)
    for kind in range(2, 4):
        for p in range(1, KV):
            returned(kind, lax.rem(j + p, KV))
    for h in range(KV):
        stage[pl.ds(h, TOK, stride=KV), :] = dkrecv[h].astype(F32)
    dk_out[...] = rope_back(stage[...].reshape(TOK, KV, DH)).astype(BF16)
    for h in range(KV):
        stage[pl.ds(h, TOK, stride=KV), :] = dvrecv[h].astype(F32)
    dv_out[...] = stage[...].reshape(TOK, KV, DH).astype(BF16)

    for p in range(1, KV):
        peer = lax.rem(j + p, KV)
        for kind, (src, dst) in enumerate(
            ((ksend, own_rows(kwin)), (vsend, own_rows(vwin)), (qsend, qbuf.at[j]), (gsend, gbuf.at[j]))
        ):
            line_copy(kind, src.at[peer], dst, peer, j, (in_s, in_r)).wait_send()
        for kind, (src, dst) in enumerate(
            ((osend, orecv), (dqsend, dqrecv), (dksend, dkrecv), (dvsend, dvrecv))
        ):
            line_copy(kind, src.at[peer], dst.at[j], peer, j, (out_s, out_r)).wait_send()
    for d in range(1, WIN + 1):
        for which in range(2):
            for h in range(2):
                @pl.when((s >= d - 1) & (s < lines - 1))
                def _():
                    hop(which, d, h).wait_send()

                @pl.when(s >= d)
                def _():
                    back(which, d, h).wait_send()


def rope_tables(positions):
    half = DH // 2
    exponent = jnp.arange(half, dtype=F32) * (2.0 / DH)
    frequency = jnp.power(jnp.float32(ROPE_BASE), -exponent)
    angle = positions.astype(F32)[:, None] * frequency[None, :]
    cosine, sine = jnp.cos(angle), jnp.sin(angle)
    return jnp.concatenate([cosine, cosine], axis=1), jnp.concatenate([-sine, sine], axis=1)


def body(lines, q_heads, k_heads, v_heads, d_out, positions, subtree_end, ancestors):
    cosine, sine = rope_tables(positions)
    ends = subtree_end.reshape(-1, BLK)
    vmem = pl.BlockSpec(memory_space=pltpu.VMEM)
    smem = pl.BlockSpec(memory_space=pltpu.SMEM)
    slab = pltpu.VMEM((KV, TOK, DH), BF16)
    rows = pltpu.VMEM((KV, ROWS, DH), BF16)
    window = pltpu.VMEM((2 * WIN + 2, BLK, DH), BF16)
    dma = pltpu.SemaphoreType.DMA
    return pl.pallas_call(
        functools.partial(kernel, lines),
        out_shape=(
            jax.ShapeDtypeStruct(q_heads.shape, BF16),
            jax.ShapeDtypeStruct(q_heads.shape, BF16),
            jax.ShapeDtypeStruct(k_heads.shape, BF16),
            jax.ShapeDtypeStruct(v_heads.shape, BF16),
        ),
        in_specs=[vmem] * 6 + [smem, vmem],
        out_specs=(vmem,) * 4,
        scratch_shapes=[
            pltpu.VMEM((ROWS, DH), F32),
            slab, slab,
            rows, rows, rows, rows,
            window, window,
            pltpu.VMEM((2, KEYS, DH), BF16),
            pltpu.VMEM((2, KEYS, DH), BF16),
            pltpu.VMEM((2, DH, KEYS), BF16),
            pltpu.VMEM((2, DH, KEYS), BF16),
            pltpu.VMEM((KV, KEYS, ROWS), F32),
            pltpu.VMEM((8, 128), F32),
            pltpu.VMEM((16, 128), BF16),
            pltpu.VMEM((2 * ANC + 1, BLK, DH), F32),
            pltpu.VMEM((2 * ANC + 1, BLK, DH), F32),
            rows, rows, rows, rows,
            pltpu.VMEM((2, 2, BLK, DH), F32),
            pltpu.VMEM((2, 2 * WIN + 2, BLK, DH), BF16),
            pltpu.VMEM((2, 2 * WIN, BLK, DH), BF16),
            slab, slab, slab, slab,
            dma((4, KV)), dma((4, KV)),
            dma((4, WIN + 1)), dma((4, WIN + 1)),
            dma((4, WIN + 1)), dma((4, WIN + 1)),
            dma((4, KV)), dma((4, KV)),
        ],
        compiler_params=pltpu.CompilerParams(
            collective_id=0, has_side_effects=True, vmem_limit_bytes=56 << 20
        ),
        cost_estimate=pl.CostEstimate(
            flops=2 * 5 * KV * KEYS * ROWS * DH, bytes_accessed=4 << 20, transcendentals=KV * KEYS * ROWS
        ),
    )(q_heads, k_heads, v_heads, d_out, cosine, sine, ancestors, ends)


def solution(mesh):
    token = P(("seq", "kv"), None, None)
    return jax.shard_map(
        functools.partial(body, mesh.shape["seq"]),
        mesh=mesh,
        in_specs=(token, token, token, token, P(("seq", "kv")), P(), P("seq", None)),
        out_specs=(token, token, token, token),
        check_vma=False,
    )
```

time: 403 us -> 92.2 us (0.23)
  the two profiles are of different devices: /device:TPU:8 before, /device:TPU:25 now
where the time goes in v1:
time: 92.2 us; the launch traced here: 92 us
  Pallas kernels  85.5 us (93%)
  local copies, waits for them, and re-layouts  4.93 us (5%)
    pallas_call x1, Pallas kernels, body(): pl.pallas_call(functools.partial(kernel, lines), out_shape=(jax.ShapeDtyp...  85.5 us
    unnamed x12, local copies, waits for them, and re-layouts  4.93 us

profile of v1, /device:TPU:25, one launch (start us, length us, event | category | flops | bytes accessed | tf_op | source)
XLA Modules:
  0.0 92.0 jit_solution(3150559902266950463)
XLA Ops:
  0.6 0.0 copy-start.3
  0.6 0.6 copy-done.3
  1.3 0.1 fusion
  1.5 0.7 pad_maximum_fusion
  2.1 85.5 %shard_map.102 = (bf16[32,64,128]{2,1,0:T(8,128)(2,1)}, bf16[32,64,128]{2,1,0:T(8,128)(2,1)}, bf16[32,8,128]{2,1,0:T(8,128)(2,1)}, bf16[32,8,128]{2,1,0:T(8,128)(2,1)}) custom-call(bf16[32,64,128]{2,1,0:T(8,128)(2,1)} %q_ref.1, bf16[32,8,128]{2,1,0:T(8,128)(2,1)} %k_ref.1, bf16[32,8,128]{2,1,0:T(8,128)(2,1)} %v_ref.1, bf16[32,64,128]{2,1,0:T(8,128)(2,1)} %g_ref.1, ...), custom_call_target="tpu_custom_call" | custom-call | flops 2013265920 | bytes 4194304 | tf_op jit(solution)/shard_map/pallas_call | solution.py:324
  87.7 0.0 copy-start
  87.7 1.9 %copy.15 = bf16[32,64,128]{2,1,0:T(8,128)(2,1)} copy(bf16[32,64,128]{2,1,0:T(8,128)(2,1)} %get-tuple-element.13) | data formatting | bytes 1048576
  89.6 0.0 copy-done
  89.6 0.0 copy-start.2
  89.6 0.8 copy.16
  90.4 0.1 copy-done.2
  90.5 0.0 copy-start.1
  90.5 0.6 copy.17
  91.1 0.2 copy-done.1
  91.3 0.6 copy.18
  (2 shorter events, 0.0 us)
Async XLA Ops:
  0.6 0.7 copy-start.3
  87.7 1.9 %copy-start = (bf16[32,64,128]{2,1,0:T(8,128)(2,1)S(1)}, bf16[32,64,128]{2,1,0:T(8,128)(2,1)}, u32[]{:S(2)}) copy-start(bf16[32,64,128]{2,1,0:T(8,128)(2,1)} %get-tuple-element.14) | copy-start | bytes 1572868
  89.6 0.9 copy-start.2
  90.5 0.9 copy-start.1

commit v2 on v1

v2 whole, which is shorter than its diff:
```python
import functools
import math

import jax
import jax.numpy as jnp
import numpy as np
from jax import lax
from jax.experimental import pallas as pl
from jax.experimental.pallas import tpu as pltpu
from jax.sharding import PartitionSpec as P

MESH = pl.DeviceIdType.MESH
BF16, F32 = jnp.bfloat16, jnp.float32
BLK = 128
ANC = 6
WIN = 7
KV = 8
GRP = 8
TOK = 32
DH = 128
ROWS = TOK * GRP
KEYS = ANC * BLK
ROPE_BASE = 500000.0
HIDDEN = -1e30
SCALE = 1.0 / math.sqrt(DH)
LOG2E = 1.4426950408889634
NT = (((1,), (1,)), ((), ()))
NN = (((1,), (0,)), ((), ()))


def dot(a, b, dims=NN):
    return lax.dot_general(a, b, dims, preferred_element_type=F32)


def kernel(
    lines,
    q_ref, k_ref, v_ref, g_ref, pos_ref, freq_ref, anc_ref, end_ref,
    o_out, dq_out, dk_out, dv_out,
    cos_ref, sin_ref, stage, ksend, vsend, qsend, gsend, qbuf, gbuf, kwin, vwin,
    kb, vb, kbt, vbt, bias, prob, plow, dka, dva,
    osend, dqsend, orecv, dqrecv, tmp, gout, gin, dsend, drecv, ofin, dqfin, dkfin, dvfin,
    line_s, line_r, next_s, next_r, win_s, win_r, grad_s, grad_r, fin,
):
    s = lax.axis_index("seq")
    j = lax.axis_index("kv")
    left, right = s - 1, s + 1
    has_left, has_right = s > 0, s < lines - 1

    barrier = pltpu.get_barrier_semaphore()

    def greet(line, peer):
        pl.semaphore_signal(barrier, inc=1, device_id=(line, peer), device_id_type=MESH)

    for p in range(1, KV):
        greet(s, lax.rem(j + p, KV))

    @pl.when(has_left)
    def _():
        for p in range(KV):
            greet(left, lax.rem(j + p, KV))

    @pl.when(has_right)
    def _():
        for p in range(KV):
            greet(right, lax.rem(j + p, KV))

    stage[...] = v_ref[...].astype(F32).reshape(ROWS, DH)
    for h in range(KV):
        vsend[h] = stage[pl.ds(h, TOK, stride=KV), :].astype(BF16)

    across = jnp.broadcast_to(pos_ref[...].astype(F32), (TOK, TOK))
    row = lax.broadcasted_iota(jnp.int32, (TOK, TOK), 0)
    lane = lax.broadcasted_iota(jnp.int32, (TOK, TOK), 1)
    position = jnp.sum(jnp.where(row == lane, across, 0.0), axis=1, keepdims=True)
    angle = position * freq_ref[...]
    lane = lax.broadcasted_iota(jnp.int32, (TOK, DH), 1)
    cos_ref[...] = jnp.cos(angle)
    sin_ref[...] = jnp.where(lane < DH // 2, -1.0, 1.0) * jnp.sin(angle)

    def rope(x):
        return x * cos_ref[...][:, None, :] + pltpu.roll(x, DH // 2, 2) * sin_ref[...][:, None, :]

    def rope_back(x):
        return x * cos_ref[...][:, None, :] - pltpu.roll(x, DH // 2, 2) * sin_ref[...][:, None, :]

    stage[...] = rope(k_ref[...].astype(F32)).reshape(ROWS, DH)
    for h in range(KV):
        ksend[h] = stage[pl.ds(h, TOK, stride=KV), :].astype(BF16)

    pl.semaphore_wait(
        barrier, KV - 1 + KV * has_left.astype(jnp.int32) + KV * has_right.astype(jnp.int32)
    )

    def line_copy(kind, src, dst, peer, slot):
        return pltpu.make_async_remote_copy(
            src_ref=src, dst_ref=dst, send_sem=line_s.at[kind, peer],
            recv_sem=line_r.at[kind, slot], device_id=(s, peer), device_id_type=MESH,
        )

    def next_copy(kind, src, dst, line, peer, slot):
        return pltpu.make_async_remote_copy(
            src_ref=src, dst_ref=dst, send_sem=next_s.at[kind, peer],
            recv_sem=next_r.at[kind, slot], device_id=(line, peer), device_id_type=MESH,
        )

    mine = pl.ds(pl.multiple_of(lax.rem(j, 4) * TOK, TOK), TOK)

    slabs, wins = (ksend, vsend), (kwin, vwin)

    def kv_here(which, peer, slot):
        return line_copy(which, slabs[which].at[peer], wins[which].at[j // 4, mine], peer, slot)

    def kv_next(which, peer, slot):
        return next_copy(which, slabs[which].at[peer], wins[which].at[2 + j // 4, mine], right, peer, slot)

    @pl.when(has_right)
    def _():
        for which in range(2):
            for p in range(KV):
                peer = lax.rem(j + p, KV)
                kv_next(which, peer, j).start()

    for which in range(2):
        for p in range(1, KV):
            peer = lax.rem(j + p, KV)
            kv_here(which, peer, j).start()
        wins[which][j // 4, mine, :] = slabs[which][j]

    for pair in range(KV // 2):
        x = q_ref[:, pair * 16:(pair + 1) * 16, :].astype(F32).reshape(TOK, 2, GRP, DH)
        y = g_ref[:, pair * 16:(pair + 1) * 16, :].astype(F32).reshape(TOK, 2, GRP, DH)
        for u in range(2):
            qsend[2 * pair + u] = rope(x[:, u]).reshape(ROWS, DH).astype(BF16)
            gsend[2 * pair + u] = y[:, u].reshape(ROWS, DH).astype(BF16)
    for p in range(1, KV):
        peer = lax.rem(j + p, KV)
        line_copy(2, qsend.at[peer], qbuf.at[j], peer, j).start()
        line_copy(3, gsend.at[peer], gbuf.at[j], peer, j).start()
    qbuf[j] = qsend[j]
    gbuf[j] = gsend[j]

    def hop(which, d, h):
        return pltpu.make_async_remote_copy(
            src_ref=wins[which].at[2 * (d - 1) + h], dst_ref=wins[which].at[2 * d + h],
            send_sem=win_s.at[2 * which + h, d], recv_sem=win_r.at[2 * which + h, d],
            device_id=(right, j), device_id_type=MESH,
        )

    for d in range(2, WIN + 1):
        for which in range(2):
            for h in range(2):
                if d > 2:
                    @pl.when(s >= d - 1)
                    def _():
                        hop(which, d - 1, h).wait_recv()
                else:
                    @pl.when(has_left)
                    def _():
                        for r in range(4):
                            kv_next(which, 4 * h + r, 4 * h + r).wait_recv()

                @pl.when((s >= d - 1) & has_right)
                def _():
                    hop(which, d, h).start()
        if d == 2:
            def mask_step(u, carry):
                b = u // ANC
                slot = lax.rem(u, ANC)
                a = anc_ref[b, slot]
                ends = end_ref[pl.ds(jnp.maximum(a, 0), 1), :].astype(F32)
                last = jnp.broadcast_to(ends, (BLK, BLK)).T
                last = jnp.where(a >= 0, last, -1.0)
                first = (a * BLK + lax.broadcasted_iota(jnp.int32, (BLK, BLK), 0)).astype(F32)
                token = lax.broadcasted_iota(jnp.int32, (BLK, BLK), 1) // GRP
                for c in range(4):
                    for half in range(2):
                        query = ((2 * s + b) * BLK + c * TOK + half * (TOK // 2) + token).astype(F32)
                        seen = (query >= first) & (query <= last)
                        bias[4 * b + c, pl.ds(pl.multiple_of(slot * BLK, BLK), BLK),
                             half * BLK:(half + 1) * BLK] = jnp.where(seen, 0.0, HIDDEN)
                return carry

            lax.fori_loop(0, 2 * ANC, mask_step, 0)
            dka[...] = jnp.zeros_like(dka)
            dva[...] = jnp.zeros_like(dva)

    def last_hop(which):
        for h in range(2):
            @pl.when(s >= WIN)
            def _():
                hop(which, WIN, h).wait_recv()

    def gather(which, block, turned):
        def step(u, carry):
            b = u // ANC
            slot = lax.rem(u, ANC)
            a = anc_ref[b, slot]
            index = 2 * (s - lax.shift_right_arithmetic(a, 1)) + (a & 1)
            index = jnp.where(a >= 0, jnp.clip(index, 0, 2 * WIN + 1), 0)
            rows = pl.ds(pl.multiple_of(slot * BLK, BLK), BLK)
            entry = wins[which][index]
            block[b, rows, :] = entry
            turned[b, :, rows] = entry.astype(F32).T.astype(BF16)
            return carry

        lax.fori_loop(0, 2 * ANC, step, 0)

    for p in range(1, KV):
        peer = lax.rem(j + p, KV)
        kv_here(0, peer, peer).wait_recv()
        kv_here(1, peer, peer).wait_recv()
    last_hop(0)
    gather(0, kb, kbt)
    for p in range(1, KV):
        peer = lax.rem(j + p, KV)
        line_copy(2, qsend.at[peer], qbuf.at[j], peer, peer).wait_recv()
        line_copy(3, gsend.at[peer], gbuf.at[j], peer, peer).wait_recv()

    def forward(p, carry):
        i = lax.rem(j + p, KV)
        b = i // 4
        scores = dot(kb[b], qbuf[i], NT) * (SCALE * LOG2E) + bias[i]
        top = jnp.max(scores, axis=0, keepdims=True)
        weight = jnp.exp2(scores - top)
        weight = weight * (1.0 / jnp.sum(weight, axis=0, keepdims=True))
        prob[i] = weight
        low = weight.astype(BF16)
        plow[i] = low
        dva[pl.ds(b * ANC, ANC)] += dot(low, gbuf[i]).reshape(ANC, BLK, DH)
        return carry

    lax.fori_loop(1, KV + 1, forward, 0)

    def back(which, d, h):
        return pltpu.make_async_remote_copy(
            src_ref=gout.at[which, 2 * d + h], dst_ref=gin.at[which, 2 * (d - 1) + h],
            send_sem=grad_s.at[2 * which + h, d], recv_sem=grad_r.at[2 * which + h, d - 1],
            device_id=(left, j), device_id_type=MESH,
        )

    def place(b, block):
        index = 2 * ANC
        for slot in range(ANC):
            hit = (anc_ref[b, slot] == block) & (block >= 0)
            index = jnp.where(hit, b * ANC + slot, index)
        return index

    def grad_step(which, d):
        acc = (dka, dva)[which]
        for h in range(2):
            block = 2 * (s - d) + h
            tmp[h] = acc[place(0, block)] + acc[place(1, block)]
            if 0 < d < WIN:
                @pl.when((s >= d) & has_right)
                def _():
                    back(which, d + 1, h).wait_recv()
                    tmp[h] = tmp[h] + gin[which, 2 * d + h].astype(F32)
            if d > 1:
                @pl.when(s >= d)
                def _():
                    gout[which, 2 * d + h] = tmp[h].astype(BF16)
                    back(which, d, h).start()
            else:
                for r in range(4):
                    dsend[d, 4 * h + r, which] = tmp[h, r * TOK:(r + 1) * TOK, :].astype(BF16)

    def backward(p, carry):
        i = lax.rem(j + p, KV)
        b = i // 4
        low, cotangent = plow[i], gbuf[i]
        attended = dot(vbt[b], low).astype(BF16)
        osend[i] = attended.astype(F32).T.astype(BF16)
        inner = jnp.sum(cotangent.astype(F32).T * attended.astype(F32), axis=0, keepdims=True)
        dprob = dot(vb[b], cotangent, NT)
        dscore = (prob[i] * (dprob - inner) * SCALE).astype(BF16)
        dka[pl.ds(b * ANC, ANC)] += dot(dscore, qbuf[i]).reshape(ANC, BLK, DH)
        dqsend[i] = dot(kbt[b], dscore).T.astype(BF16)

        @pl.when(i != j)
        def _():
            line_copy(4, osend.at[i], orecv.at[j], i, j).start()
            line_copy(5, dqsend.at[i], dqrecv.at[j], i, j).start()

        @pl.when(i == j)
        def _():
            orecv[j] = osend[i]
            dqrecv[j] = dqsend[i]

        return carry

    def finish(pair):
        for u in range(2):
            peer = 2 * pair + u

            @pl.when(peer != j)
            def _():
                line_copy(4, osend.at[peer], orecv.at[j], peer, peer).wait_recv()
                line_copy(5, dqsend.at[peer], dqrecv.at[j], peer, peer).wait_recv()
        heads = slice(pair * 16, (pair + 1) * 16)
        x = [orecv[2 * pair + u].astype(F32).reshape(TOK, GRP, DH) for u in range(2)]
        ofin[:, heads, :] = jnp.concatenate(x, axis=1).astype(BF16)
        x = [rope_back(dqrecv[2 * pair + u].astype(F32).reshape(TOK, GRP, DH)) for u in range(2)]
        dqfin[:, heads, :] = jnp.concatenate(x, axis=1).astype(BF16)

    grad_step(1, WIN)
    last_hop(1)
    gather(1, vb, vbt)
    lax.fori_loop(1, KV // 2 + 1, backward, 0)
    grad_step(1, WIN - 1)
    lax.fori_loop(KV // 2 + 1, KV + 1, backward, 0)
    grad_step(0, WIN)
    grad_step(1, WIN - 2)
    grad_step(0, 0)
    grad_step(1, 0)

    def d_here(peer, slot):
        return line_copy(6, dsend.at[0, peer], drecv.at[0, j], peer, slot)

    def d_next(peer, slot):
        return next_copy(2, dsend.at[1, peer], drecv.at[1, j], left, peer, slot)

    for p in range(1, KV):
        peer = lax.rem(j + p, KV)
        d_here(peer, j).start()
    drecv[0, j] = dsend[0, j]

    for d in range(WIN - 1, 0, -1):
        grad_step(0, d)
        if d > 2:
            grad_step(1, d - 2)
        if d in (2, 3):
            finish(3 - d)

    @pl.when(has_left)
    def _():
        for p in range(KV):
            peer = lax.rem(j + p, KV)
            d_next(peer, j).start()

    finish(2)
    finish(3)
    done = [pltpu.make_async_copy(ofin, o_out, fin.at[0]), pltpu.make_async_copy(dqfin, dq_out, fin.at[1]),
            pltpu.make_async_copy(dkfin, dk_out, fin.at[2]), pltpu.make_async_copy(dvfin, dv_out, fin.at[3])]
    done[0].start()
    done[1].start()
    for p in range(1, KV):
        peer = lax.rem(j + p, KV)
        d_here(peer, peer).wait_recv()

    @pl.when(has_right)
    def _():
        for p in range(KV):
            d_next(p, p).wait_recv()

    @pl.when(jnp.logical_not(has_right))
    def _():
        drecv[1] = jnp.zeros_like(drecv[1])

    for which in range(2):
        for h in range(KV):
            total = drecv[0, h, which].astype(F32) + drecv[1, h, which].astype(F32)
            stage[pl.ds(h, TOK, stride=KV), :] = total
        total = stage[...].reshape(TOK, KV, DH).astype(BF16)
        if which == 0:
            dkfin[...] = rope_back(total.astype(F32)).astype(BF16)
        else:
            dvfin[...] = total
        done[2 + which].start()

    for p in range(1, KV):
        peer = lax.rem(j + p, KV)
        kv_here(0, peer, j).wait_send()
        kv_here(1, peer, j).wait_send()
        line_copy(2, qsend.at[peer], qbuf.at[j], peer, j).wait_send()
        line_copy(3, gsend.at[peer], gbuf.at[j], peer, j).wait_send()
        line_copy(4, osend.at[peer], orecv.at[j], peer, j).wait_send()
        line_copy(5, dqsend.at[peer], dqrecv.at[j], peer, j).wait_send()
        d_here(peer, j).wait_send()

    @pl.when(has_right)
    def _():
        for p in range(KV):
            kv_next(0, p, j).wait_send()
            kv_next(1, p, j).wait_send()

    @pl.when(has_left)
    def _():
        for p in range(KV):
            d_next(p, j).wait_send()

    for d in range(2, WIN + 1):
        for which in range(2):
            for h in range(2):
                @pl.when((s >= d - 1) & has_right)
                def _():
                    hop(which, d, h).wait_send()

                @pl.when(s >= d)
                def _():
                    back(which, d, h).wait_send()
    for copy in done:
        copy.wait()


def copy_kernel(a, b, c, d, e, f, g, h, sems):
    copies = [pltpu.make_async_copy(x, y, sems.at[n]) for n, (x, y) in enumerate(((a, e), (b, f), (c, g), (d, h)))]
    for copy in copies:
        copy.start()
    for copy in copies:
        copy.wait()


def body(lines, q_heads, k_heads, v_heads, d_out, positions, subtree_end, ancestors):
    frequency = ROPE_BASE ** (-2.0 * (np.arange(DH) % (DH // 2)) / DH)
    frequency = jnp.asarray(frequency[None, :], F32)
    vmem = pl.BlockSpec(memory_space=pltpu.VMEM)
    smem = pl.BlockSpec(memory_space=pltpu.SMEM)
    hbm = pl.BlockSpec(memory_space=pl.ANY)
    rows = pltpu.VMEM((KV, ROWS, DH), BF16)
    dma = pltpu.SemaphoreType.DMA
    shapes = tuple(jax.ShapeDtypeStruct(x.shape, BF16) for x in (q_heads, q_heads, k_heads, v_heads))
    outs = pl.pallas_call(
        functools.partial(kernel, lines),
        out_shape=shapes,
        in_specs=[vmem] * 6 + [smem, vmem],
        out_specs=(hbm,) * 4,
        scratch_shapes=[
            pltpu.VMEM((TOK, DH), F32),
            pltpu.VMEM((TOK, DH), F32),
            pltpu.VMEM((ROWS, DH), F32),
            pltpu.VMEM((KV, TOK, DH), BF16),
            pltpu.VMEM((KV, TOK, DH), BF16),
            rows, rows, rows, rows,
            pltpu.VMEM((2 * WIN + 2, BLK, DH), BF16),
            pltpu.VMEM((2 * WIN + 2, BLK, DH), BF16),
            pltpu.VMEM((2, KEYS, DH), BF16),
            pltpu.VMEM((2, KEYS, DH), BF16),
            pltpu.VMEM((2, DH, KEYS), BF16),
            pltpu.VMEM((2, DH, KEYS), BF16),
            pltpu.VMEM((KV, KEYS, ROWS), F32),
            pltpu.VMEM((KV, KEYS, ROWS), F32),
            pltpu.VMEM((KV, KEYS, ROWS), BF16),
            pltpu.VMEM((2 * ANC + 1, BLK, DH), F32),
            pltpu.VMEM((2 * ANC + 1, BLK, DH), F32),
            rows, rows, rows, rows,
            pltpu.VMEM((2, BLK, DH), F32),
            pltpu.VMEM((2, 2 * WIN + 2, BLK, DH), BF16),
            pltpu.VMEM((2, 2 * WIN, BLK, DH), BF16),
            pltpu.VMEM((2, KV, 2, TOK, DH), BF16),
            pltpu.VMEM((2, KV, 2, TOK, DH), BF16),
            pltpu.VMEM(q_heads.shape, BF16),
            pltpu.VMEM(q_heads.shape, BF16),
            pltpu.VMEM(k_heads.shape, BF16),
            pltpu.VMEM(k_heads.shape, BF16),
            dma((7, KV)), dma((7, KV)),
            dma((3, KV)), dma((3, KV)),
            dma((4, WIN + 1)), dma((4, WIN + 1)),
            dma((4, WIN + 1)), dma((4, WIN + 1)),
            dma((4,)),
        ],
        compiler_params=pltpu.CompilerParams(
            collective_id=0, has_side_effects=True, vmem_limit_bytes=56 << 20
        ),
        cost_estimate=pl.CostEstimate(
            flops=2 * 5 * KV * KEYS * ROWS * DH, bytes_accessed=4 << 20, transcendentals=KV * KEYS * ROWS
        ),
    )(q_heads, k_heads, v_heads, d_out, positions.reshape(1, TOK), frequency, ancestors, subtree_end.reshape(-1, BLK))
    return pl.pallas_call(
        copy_kernel,
        out_shape=shapes,
        in_specs=[vmem] * 4,
        out_specs=(hbm,) * 4,
        scratch_shapes=[dma((4,))],
    )(*outs)


def solution(mesh):
    token = P(("seq", "kv"), None, None)
    return jax.shard_map(
        functools.partial(body, mesh.shape["seq"]),
        mesh=mesh,
        in_specs=(token, token, token, token, P(("seq", "kv")), P(), P("seq", None)),
        out_specs=(token, token, token, token),
        check_vma=False,
    )
```

time: 92.2 us -> 85.1 us (0.923)
  local copies, waits for them, and re-layouts: 4.93 us -> 0 us
  Pallas kernels: 85.5 us -> 84.3 us
    unnamed x12 -> x0, local copies, waits for them, and re-layouts: 4.93 us -> none
    pallas_call x1 -> x2, Pallas kernels: 85.5 us -> 84.3 us  [the longest x1 82.1 us: body(): pl.pallas_call(functools.partial(kernel, lines), out_shape=shapes, in_spe...]
where the time goes in v2:
time: 85.1 us; the launch traced here: 85 us
  Pallas kernels  84.3 us (99%)
    pallas_call x1, Pallas kernels, body(): pl.pallas_call(functools.partial(kernel, lines), out_shape=shapes, in_spe...  82.1 us
    pallas_call x1, Pallas kernels, body(): pl.pallas_call(copy_kernel, out_shape=shapes, in_specs=[vmem] * 4, out_sp...  2.24 us

profile of v2, /device:TPU:25, one launch (start us, length us, event | category | flops | bytes accessed | tf_op | source)
XLA Modules:
  0.0 85.0 jit_solution(15367093376937258286)
XLA Ops:
  0.6 82.1 %shard_map.111 = (bf16[32,64,128]{2,1,0:T(8,128)(2,1)}, bf16[32,64,128]{2,1,0:T(8,128)(2,1)}, bf16[32,8,128]{2,1,0:T(8,128)(2,1)}, bf16[32,8,128]{2,1,0:T(8,128)(2,1)}) custom-call(bf16[32,64,128]{2,1,0:T(8,128)(2,1)} %q_ref.1, bf16[32,8,128]{2,1,0:T(8,128)(2,1)} %k_ref.1, bf16[32,8,128]{2,1,0:T(8,128)(2,1)} %v_ref.1, bf16[32,64,128]{2,1,0:T(8,128)(2,1)} %g_ref.1, ...), custom_call_target="tpu_custom_call" | custom-call | flops 2013265920 | bytes 4194304 | tf_op jit(solution)/shard_map/pallas_call | solution.py:422
  82.7 2.2 %shard_map.112 = (bf16[32,64,128]{2,1,0:T(8,128)(2,1)}, bf16[32,64,128]{2,1,0:T(8,128)(2,1)}, bf16[32,8,128]{2,1,0:T(8,128)(2,1)}, bf16[32,8,128]{2,1,0:T(8,128)(2,1)}) custom-call(bf16[32,64,128]{2,1,0:T(8,128)(2,1)} %get-tuple-element.8.a, bf16[32,64,128]{2,1,0:T(8,128)(2,1)} %get-tuple-element.9.b, bf16[32,8,128]{2,1,0:T(8,128)(2,1)} %get-tuple-element.10.c, ...), custom_call_target="tpu_custom_call" | custom-call | tf_op jit(solution)/shard_map/pallas_call | solution.py:468

commit v3 on v2

--- a/solution.py
+++ b/solution.py
@@ -34,18 +34,28 @@
 
 def kernel(
     lines,
-    q_ref, k_ref, v_ref, g_ref, pos_ref, freq_ref, anc_ref, end_ref,
+    q_in, k_in, v_in, g_in, pos_in, freq_in, anc_in, end_in,
     o_out, dq_out, dk_out, dv_out,
-    cos_ref, sin_ref, stage, ksend, vsend, qsend, gsend, qbuf, gbuf, kwin, vwin,
-    kb, vb, kbt, vbt, bias, prob, plow, dka, dva,
+    q_ref, k_ref, v_ref, g_ref, pos_ref, freq_ref, anc_ref, end_ref, cos_ref, sin_ref, stage, ksend, vsend, qsend, gsend, qbuf, gbuf, kwin, vwin,
+    kb, vb, kbt, vbt, bias, prob, plow, work, dlow, norm, dka, dva,
     osend, dqsend, orecv, dqrecv, tmp, gout, gin, dsend, drecv, ofin, dqfin, dkfin, dvfin,
-    line_s, line_r, next_s, next_r, win_s, win_r, grad_s, grad_r, fin,
+    line_s, line_r, next_s, next_r, win_s, win_r, grad_s, grad_r, fin, load,
 ):
     s = lax.axis_index("seq")
     j = lax.axis_index("kv")
     left, right = s - 1, s + 1
     has_left, has_right = s > 0, s < lines - 1
 
+    loads = [
+        pltpu.make_async_copy(src, dst, load.at[n])
+        for n, (src, dst) in enumerate((
+            (v_in, v_ref), (pos_in, pos_ref), (freq_in, freq_ref), (k_in, k_ref),
+            (q_in, q_ref), (g_in, g_ref), (end_in, end_ref), (anc_in, anc_ref),
+        ))
+    ]
+    for copy in loads:
+        copy.start()
+
     barrier = pltpu.get_barrier_semaphore()
 
     def greet(line, peer):
@@ -64,6 +74,8 @@
         for p in range(KV):
             greet(right, lax.rem(j + p, KV))
 
+    for copy in loads[:4]:
+        copy.wait()
     stage[...] = v_ref[...].astype(F32).reshape(ROWS, DH)
     for h in range(KV):
         vsend[h] = stage[pl.ds(h, TOK, stride=KV), :].astype(BF16)
@@ -87,44 +99,8 @@
     for h in range(KV):
         ksend[h] = stage[pl.ds(h, TOK, stride=KV), :].astype(BF16)
 
-    pl.semaphore_wait(
-        barrier, KV - 1 + KV * has_left.astype(jnp.int32) + KV * has_right.astype(jnp.int32)
-    )
-
-    def line_copy(kind, src, dst, peer, slot):
-        return pltpu.make_async_remote_copy(
-            src_ref=src, dst_ref=dst, send_sem=line_s.at[kind, peer],
-            recv_sem=line_r.at[kind, slot], device_id=(s, peer), device_id_type=MESH,
-        )
-
-    def next_copy(kind, src, dst, line, peer, slot):
-        return pltpu.make_async_remote_copy(
-            src_ref=src, dst_ref=dst, send_sem=next_s.at[kind, peer],
-            recv_sem=next_r.at[kind, slot], device_id=(line, peer), device_id_type=MESH,
-        )
-
-    mine = pl.ds(pl.multiple_of(lax.rem(j, 4) * TOK, TOK), TOK)
-
-    slabs, wins = (ksend, vsend), (kwin, vwin)
-
-    def kv_here(which, peer, slot):
-        return line_copy(which, slabs[which].at[peer], wins[which].at[j // 4, mine], peer, slot)
-
-    def kv_next(which, peer, slot):
-        return next_copy(which, slabs[which].at[peer], wins[which].at[2 + j // 4, mine], right, peer, slot)
-
-    @pl.when(has_right)
-    def _():
-        for which in range(2):
-            for p in range(KV):
-                peer = lax.rem(j + p, KV)
-                kv_next(which, peer, j).start()
-
-    for which in range(2):
-        for p in range(1, KV):
-            peer = lax.rem(j + p, KV)
-            kv_here(which, peer, j).start()
-        wins[which][j // 4, mine, :] = slabs[which][j]
+    for copy in loads[4:]:
+        copy.wait()
 
     for pair in range(KV // 2):
         x = q_ref[:, pair * 16:(pair + 1) * 16, :].astype(F32).reshape(TOK, 2, GRP, DH)
@@ -132,17 +108,61 @@
         for u in range(2):
             qsend[2 * pair + u] = rope(x[:, u]).reshape(ROWS, DH).astype(BF16)
             gsend[2 * pair + u] = y[:, u].reshape(ROWS, DH).astype(BF16)
+
+    pl.semaphore_wait(
+        barrier, KV - 1 + KV * has_left.astype(jnp.int32) + KV * has_right.astype(jnp.int32)
+    )
+
+    def line_copy(kind, src, dst, peer):
+        return pltpu.make_async_remote_copy(
+            src_ref=src, dst_ref=dst, send_sem=line_s.at[kind],
+            recv_sem=line_r.at[kind], device_id=(s, peer), device_id_type=MESH,
+        )
+
+    def next_copy(kind, slot, src, dst, line, peer):
+        return pltpu.make_async_remote_copy(
+            src_ref=src, dst_ref=dst, send_sem=next_s.at[kind],
+            recv_sem=next_r.at[slot], device_id=(line, peer), device_id_type=MESH,
+        )
+
+    others = pl.ds(0, KV - 1)
+
+    mine = pl.ds(pl.multiple_of(lax.rem(j, 4) * TOK, TOK), TOK)
+
+    slabs, wins = (ksend, vsend), (kwin, vwin)
+
+    def kv_here(which, peer):
+        return line_copy(which, slabs[which].at[peer], wins[which].at[j // 4, mine], peer)
+
+    def kv_next(which, peer):
+        return next_copy(
+            which, 2 * which + j // 4, slabs[which].at[peer], wins[which].at[2 + j // 4, mine], right, peer
+        )
+
+    @pl.when(has_right)
+    def _():
+        for which in range(2):
+            for p in range(KV):
+                peer = lax.rem(j + p, KV)
+                kv_next(which, peer).start()
+
+    for which in range(2):
+        for p in range(1, KV):
+            peer = lax.rem(j + p, KV)
+            kv_here(which, peer).start()
+        wins[which][j // 4, mine, :] = slabs[which][j]
+
     for p in range(1, KV):
         peer = lax.rem(j + p, KV)
-        line_copy(2, qsend.at[peer], qbuf.at[j], peer, j).start()
-        line_copy(3, gsend.at[peer], gbuf.at[j], peer, j).start()
+        line_copy(2, qsend.at[peer], qbuf.at[j], peer).start()
+        line_copy(3, gsend.at[peer], gbuf.at[j], peer).start()
     qbuf[j] = qsend[j]
     gbuf[j] = gsend[j]
 
     def hop(which, d, h):
         return pltpu.make_async_remote_copy(
             src_ref=wins[which].at[2 * (d - 1) + h], dst_ref=wins[which].at[2 * d + h],
-            send_sem=win_s.at[2 * which + h, d], recv_sem=win_r.at[2 * which + h, d],
+            send_sem=win_s.at[which], recv_sem=win_r.at[2 * which + h, d - 2],
             device_id=(right, j), device_id_type=MESH,
         )
 
@@ -156,8 +176,8 @@
                 else:
                     @pl.when(has_left)
                     def _():
-                        for r in range(4):
-                            kv_next(which, 4 * h + r, 4 * h + r).wait_recv()
+                        half = wins[which].at[2 + h]
+                        next_copy(which, 2 * which + h, half, half, right, j).wait_recv()
 
                 @pl.when((s >= d - 1) & has_right)
                 def _():
@@ -205,28 +225,35 @@
 
         lax.fori_loop(0, 2 * ANC, step, 0)
 
-    for p in range(1, KV):
-        peer = lax.rem(j + p, KV)
-        kv_here(0, peer, peer).wait_recv()
-        kv_here(1, peer, peer).wait_recv()
+    for which in range(2):
+        line_copy(which, slabs[which].at[others], slabs[which].at[others], j).wait_recv()
     last_hop(0)
     gather(0, kb, kbt)
-    for p in range(1, KV):
-        peer = lax.rem(j + p, KV)
-        line_copy(2, qsend.at[peer], qbuf.at[j], peer, peer).wait_recv()
-        line_copy(3, gsend.at[peer], gbuf.at[j], peer, peer).wait_recv()
+    line_copy(2, qsend.at[others], qbuf.at[others], j).wait_recv()
+    line_copy(3, gsend.at[others], gbuf.at[others], j).wait_recv()
 
     def forward(p, carry):
         i = lax.rem(j + p, KV)
         b = i // 4
-        scores = dot(kb[b], qbuf[i], NT) * (SCALE * LOG2E) + bias[i]
-        top = jnp.max(scores, axis=0, keepdims=True)
-        weight = jnp.exp2(scores - top)
-        weight = weight * (1.0 / jnp.sum(weight, axis=0, keepdims=True))
-        prob[i] = weight
-        low = weight.astype(BF16)
-        plow[i] = low
-        dva[pl.ds(b * ANC, ANC)] += dot(low, gbuf[i]).reshape(ANC, BLK, DH)
+        slots = [slice(n * BLK, (n + 1) * BLK) for n in range(ANC)]
+        work[...] = dot(kb[b], qbuf[i], NT)
+
+        def score(n):
+            return work[slots[n], :] * (SCALE * LOG2E) + bias[i, slots[n], :]
+
+        top = jnp.max(score(0), axis=0, keepdims=True)
+        for n in range(1, ANC):
+            top = jnp.maximum(top, jnp.max(score(n), axis=0, keepdims=True))
+        total = jnp.zeros((1, ROWS), F32)
+        for n in range(ANC):
+            weight = jnp.exp2(score(n) - top)
+            prob[i, slots[n], :] = weight
+            total = total + jnp.sum(weight, axis=0, keepdims=True)
+        share = 1.0 / total
+        norm[i] = share
+        for n in range(ANC):
+            plow[i, slots[n], :] = (prob[i, slots[n], :] * share).astype(BF16)
+        dva[pl.ds(b * ANC, ANC)] += dot(plow[i], gbuf[i]).reshape(ANC, BLK, DH)
         return carry
 
     lax.fori_loop(1, KV + 1, forward, 0)
@@ -234,7 +261,7 @@
     def back(which, d, h):
         return pltpu.make_async_remote_copy(
             src_ref=gout.at[which, 2 * d + h], dst_ref=gin.at[which, 2 * (d - 1) + h],
-            send_sem=grad_s.at[2 * which + h, d], recv_sem=grad_r.at[2 * which + h, d - 1],
+            send_sem=grad_s.at[which], recv_sem=grad_r.at[2 * which + h, d - 2],
             device_id=(left, j), device_id_type=MESH,
         )
 
@@ -271,15 +298,18 @@
         attended = dot(vbt[b], low).astype(BF16)
         osend[i] = attended.astype(F32).T.astype(BF16)
         inner = jnp.sum(cotangent.astype(F32).T * attended.astype(F32), axis=0, keepdims=True)
-        dprob = dot(vb[b], cotangent, NT)
-        dscore = (prob[i] * (dprob - inner) * SCALE).astype(BF16)
-        dka[pl.ds(b * ANC, ANC)] += dot(dscore, qbuf[i]).reshape(ANC, BLK, DH)
-        dqsend[i] = dot(kbt[b], dscore).T.astype(BF16)
+        work[...] = dot(vb[b], cotangent, NT)
+        factor = norm[i] * SCALE
+        for n in range(ANC):
+            rows = slice(n * BLK, (n + 1) * BLK)
+            dlow[rows, :] = (prob[i, rows, :] * ((work[rows, :] - inner) * factor)).astype(BF16)
+        dka[pl.ds(b * ANC, ANC)] += dot(dlow[...], qbuf[i]).reshape(ANC, BLK, DH)
+        dqsend[i] = dot(kbt[b], dlow[...]).T.astype(BF16)
 
         @pl.when(i != j)
         def _():
-            line_copy(4, osend.at[i], orecv.at[j], i, j).start()
-            line_copy(5, dqsend.at[i], dqrecv.at[j], i, j).start()
+            line_copy(4, osend.at[i], orecv.at[j], i).start()
+            line_copy(5, dqsend.at[i], dqrecv.at[j], i).start()
 
         @pl.when(i == j)
         def _():
@@ -289,13 +319,9 @@
         return carry
 
     def finish(pair):
-        for u in range(2):
-            peer = 2 * pair + u
-
-            @pl.when(peer != j)
-            def _():
-                line_copy(4, osend.at[peer], orecv.at[j], peer, peer).wait_recv()
-                line_copy(5, dqsend.at[peer], dqrecv.at[j], peer, peer).wait_recv()
+        if pair == 0:
+            line_copy(4, osend.at[others], orecv.at[others], j).wait_recv()
+            line_copy(5, dqsend.at[others], dqrecv.at[others], j).wait_recv()
         heads = slice(pair * 16, (pair + 1) * 16)
         x = [orecv[2 * pair + u].astype(F32).reshape(TOK, GRP, DH) for u in range(2)]
         ofin[:, heads, :] = jnp.concatenate(x, axis=1).astype(BF16)
@@ -313,15 +339,9 @@
     grad_step(0, 0)
     grad_step(1, 0)
 
-    def d_here(peer, slot):
-        return line_copy(6, dsend.at[0, peer], drecv.at[0, j], peer, slot)
-
-    def d_next(peer, slot):
-        return next_copy(2, dsend.at[1, peer], drecv.at[1, j], left, peer, slot)
-
     for p in range(1, KV):
         peer = lax.rem(j + p, KV)
-        d_here(peer, j).start()
+        line_copy(6, dsend.at[0, peer], drecv.at[0, j], peer).start()
     drecv[0, j] = dsend[0, j]
 
     for d in range(WIN - 1, 0, -1):
@@ -335,7 +355,7 @@
     def _():
         for p in range(KV):
             peer = lax.rem(j + p, KV)
-            d_next(peer, j).start()
+            next_copy(2, 4, dsend.at[1, peer], drecv.at[1, j], left, peer).start()
 
     finish(2)
     finish(3)
@@ -343,14 +363,11 @@
             pltpu.make_async_copy(dkfin, dk_out, fin.at[2]), pltpu.make_async_copy(dvfin, dv_out, fin.at[3])]
     done[0].start()
     done[1].start()
-    for p in range(1, KV):
-        peer = lax.rem(j + p, KV)
-        d_here(peer, peer).wait_recv()
+    line_copy(6, dsend.at[0, others], drecv.at[0, others], j).wait_recv()
 
     @pl.when(has_right)
     def _():
-        for p in range(KV):
-            d_next(p, p).wait_recv()
+        next_copy(2, 4, dsend.at[1], drecv.at[1], right, j).wait_recv()
 
     @pl.when(jnp.logical_not(has_right))
     def _():
@@ -367,54 +384,59 @@
             dvfin[...] = total
         done[2 + which].start()
 
-    for p in range(1, KV):
-        peer = lax.rem(j + p, KV)
-        kv_here(0, peer, j).wait_send()
-        kv_here(1, peer, j).wait_send()
-        line_copy(2, qsend.at[peer], qbuf.at[j], peer, j).wait_send()
-        line_copy(3, gsend.at[peer], gbuf.at[j], peer, j).wait_send()
-        line_copy(4, osend.at[peer], orecv.at[j], peer, j).wait_send()
-        line_copy(5, dqsend.at[peer], dqrecv.at[j], peer, j).wait_send()
-        d_here(peer, j).wait_send()
+    for kind, (src, dst) in enumerate((
+        (ksend, ksend), (vsend, vsend), (qsend, qbuf), (gsend, gbuf), (osend, orecv), (dqsend, dqrecv),
+        (dsend.at[0], drecv.at[0]),
+    )):
+        line_copy(kind, src.at[others], dst.at[others], j).wait_send()
 
     @pl.when(has_right)
     def _():
-        for p in range(KV):
-            kv_next(0, p, j).wait_send()
-            kv_next(1, p, j).wait_send()
+        for which in range(2):
+            next_copy(which, 2 * which, slabs[which], slabs[which], right, j).wait_send()
 
     @pl.when(has_left)
     def _():
-        for p in range(KV):
-            d_next(p, j).wait_send()
-
-    for d in range(2, WIN + 1):
-        for which in range(2):
-            for h in range(2):
-                @pl.when((s >= d - 1) & has_right)
-                def _():
-                    hop(which, d, h).wait_send()
-
-                @pl.when(s >= d)
-                def _():
-                    back(which, d, h).wait_send()
+        next_copy(2, 4, dsend.at[1], drecv.at[1], left, j).wait_send()
+
+    for n in range(1, WIN):
+        some = pl.ds(0, 2 * n)
+
+        @pl.when((s >= n if n == WIN - 1 else s == n) & has_right)
+        def _():
+            for which in range(2):
+                pltpu.make_async_remote_copy(
+                    src_ref=wins[which].at[some], dst_ref=wins[which].at[some], send_sem=win_s.at[which],
+                    recv_sem=win_r.at[0, 0], device_id=(right, j), device_id_type=MESH,
+                ).wait_send()
+
+        @pl.when(s >= n + 1 if n == WIN - 1 else s == n + 1)
+        def _():
+            for which in range(2):
+                pltpu.make_async_remote_copy(
+                    src_ref=gout.at[which, some], dst_ref=gin.at[which, some], send_sem=grad_s.at[which],
+                    recv_sem=grad_r.at[0, 0], device_id=(left, j), device_id_type=MESH,
+                ).wait_send()
     for copy in done:
         copy.wait()
 
 
-def copy_kernel(a, b, c, d, e, f, g, h, sems):
-    copies = [pltpu.make_async_copy(x, y, sems.at[n]) for n, (x, y) in enumerate(((a, e), (b, f), (c, g), (d, h)))]
-    for copy in copies:
+def copy_kernel(*refs):
+    ins, outs, mids, sems = refs[:4], refs[4:8], refs[8:12], refs[12]
+    first = [pltpu.make_async_copy(ins[n], mids[n], sems.at[0, n]) for n in range(4)]
+    second = [pltpu.make_async_copy(mids[n], outs[n], sems.at[1, n]) for n in range(4)]
+    for copy in first:
         copy.start()
-    for copy in copies:
+    for n in range(4):
+        first[n].wait()
+        second[n].start()
+    for copy in second:
         copy.wait()
 
 
 def body(lines, q_heads, k_heads, v_heads, d_out, positions, subtree_end, ancestors):
     frequency = ROPE_BASE ** (-2.0 * (np.arange(DH) % (DH // 2)) / DH)
     frequency = jnp.asarray(frequency[None, :], F32)
-    vmem = pl.BlockSpec(memory_space=pltpu.VMEM)
-    smem = pl.BlockSpec(memory_space=pltpu.SMEM)
     hbm = pl.BlockSpec(memory_space=pl.ANY)
     rows = pltpu.VMEM((KV, ROWS, DH), BF16)
     dma = pltpu.SemaphoreType.DMA
@@ -422,9 +444,17 @@
     outs = pl.pallas_call(
         functools.partial(kernel, lines),
         out_shape=shapes,
-        in_specs=[vmem] * 6 + [smem, vmem],
+        in_specs=[hbm] * 8,
         out_specs=(hbm,) * 4,
         scratch_shapes=[
+            pltpu.VMEM(q_heads.shape, BF16),
+            pltpu.VMEM(k_heads.shape, BF16),
+            pltpu.VMEM(k_heads.shape, BF16),
+            pltpu.VMEM(q_heads.shape, BF16),
+            pltpu.VMEM((1, TOK), jnp.int32),
+            pltpu.VMEM((1, DH), F32),
+            pltpu.SMEM((2, ANC), jnp.int32),
+            pltpu.VMEM((subtree_end.shape[0] // BLK, BLK), jnp.int32),
             pltpu.VMEM((TOK, DH), F32),
             pltpu.VMEM((TOK, DH), F32),
             pltpu.VMEM((ROWS, DH), F32),
@@ -440,6 +470,9 @@
             pltpu.VMEM((KV, KEYS, ROWS), F32),
             pltpu.VMEM((KV, KEYS, ROWS), F32),
             pltpu.VMEM((KV, KEYS, ROWS), BF16),
+            pltpu.VMEM((KEYS, ROWS), F32),
+            pltpu.VMEM((KEYS, ROWS), BF16),
+            pltpu.VMEM((KV, 1, ROWS), F32),
             pltpu.VMEM((2 * ANC + 1, BLK, DH), F32),
             pltpu.VMEM((2 * ANC + 1, BLK, DH), F32),
             rows, rows, rows, rows,
@@ -452,11 +485,11 @@
             pltpu.VMEM(q_heads.shape, BF16),
             pltpu.VMEM(k_heads.shape, BF16),
             pltpu.VMEM(k_heads.shape, BF16),
-            dma((7, KV)), dma((7, KV)),
-            dma((3, KV)), dma((3, KV)),
-            dma((4, WIN + 1)), dma((4, WIN + 1)),
-            dma((4, WIN + 1)), dma((4, WIN + 1)),
-            dma((4,)),
+            dma((7,)), dma((7,)),
+            dma((3,)), dma((5,)),
+            dma((2,)), dma((4, WIN - 1)),
+            dma((2,)), dma((4, WIN - 1)),
+            dma((4,)), dma((8,)),
         ],
         compiler_params=pltpu.CompilerParams(
             collective_id=0, has_side_effects=True, vmem_limit_bytes=56 << 20
@@ -468,9 +501,9 @@
     return pl.pallas_call(
         copy_kernel,
         out_shape=shapes,
-        in_specs=[vmem] * 4,
+        in_specs=[hbm] * 4,
         out_specs=(hbm,) * 4,
-        scratch_shapes=[dma((4,))],
+        scratch_shapes=[pltpu.VMEM(x.shape, BF16) for x in shapes] + [dma((2, 4))],
     )(*outs)
 
 

time: 85.1 us -> 81.3 us (0.955)
  Pallas kernels: 84.3 us -> 80.5 us
    pallas_call x1, Pallas kernels: 82.1 us -> 78.4 us  [body(): pl.pallas_call(functools.partial(kernel, lines), out_shape=shapes, in_spe...]
where the time goes in v3:
time: 81.3 us; the launch traced here: 81.1 us
  Pallas kernels  80.5 us (99%)
    pallas_call x1, Pallas kernels, body(): pl.pallas_call(functools.partial(kernel, lines), out_shape=shapes, in_spe...  78.4 us
    pallas_call x1, Pallas kernels, body(): pl.pallas_call(copy_kernel, out_shape=shapes, in_specs=[hbm] * 4, out_spe...  2.11 us

profile of v3, /device:TPU:25, one launch (start us, length us, event | category | flops | bytes accessed | tf_op | source)
XLA Modules:
  0.0 81.1 jit_solution(14174058960903774024)
XLA Ops:
  0.6 78.4 %shard_map.111 = (bf16[32,64,128]{2,1,0:T(8,128)(2,1)}, bf16[32,64,128]{2,1,0:T(8,128)(2,1)}, bf16[32,8,128]{2,1,0:T(8,128)(2,1)}, bf16[32,8,128]{2,1,0:T(8,128)(2,1)}) custom-call(bf16[32,64,128]{2,1,0:T(8,128)(2,1)} %q_in.1, bf16[32,8,128]{2,1,0:T(8,128)(2,1)} %k_in.1, bf16[32,8,128]{2,1,0:T(8,128)(2,1)} %v_in.1, bf16[32,64,128]{2,1,0:T(8,128)(2,1)} %g_in.1, ...), custom_call_target="tpu_custom_call" | custom-call | flops 2013265920 | bytes 4194304 | tf_op jit(solution)/shard_map/pallas_call | solution.py:444
  79.0 2.1 %shard_map.112 = (bf16[32,64,128]{2,1,0:T(8,128)(2,1)}, bf16[32,64,128]{2,1,0:T(8,128)(2,1)}, bf16[32,8,128]{2,1,0:T(8,128)(2,1)}, bf16[32,8,128]{2,1,0:T(8,128)(2,1)}) custom-call(bf16[32,64,128]{2,1,0:T(8,128)(2,1)} %get-tuple-element.8.refs_0_, bf16[32,64,128]{2,1,0:T(8,128)(2,1)} %get-tuple-element.9.refs_1_, ...), custom_call_target="tpu_custom_call" | custom-call | tf_op jit(solution)/shard_map/pallas_call | solution.py:501

commit v4 on v3

--- a/solution.py
+++ b/solution.py
@@ -36,7 +36,7 @@
     lines,
     q_in, k_in, v_in, g_in, pos_in, freq_in, anc_in, end_in,
     o_out, dq_out, dk_out, dv_out,
-    q_ref, k_ref, v_ref, g_ref, pos_ref, freq_ref, anc_ref, end_ref, cos_ref, sin_ref, stage, ksend, vsend, qsend, gsend, qbuf, gbuf, kwin, vwin,
+    q_ref, k_ref, v_ref, g_ref, pos_ref, freq_ref, anc_ref, end_ref, cos_ref, sin_ref, stage, ksend, vsend, qsend, gsend, qbuf, gbuf, kwin, klast, vwin,
     kb, vb, kbt, vbt, bias, prob, plow, work, dlow, norm, dka, dva,
     osend, dqsend, orecv, dqrecv, tmp, gout, gin, dsend, drecv, ofin, dqfin, dkfin, dvfin,
     line_s, line_r, next_s, next_r, win_s, win_r, grad_s, grad_r, fin, load,
@@ -160,8 +160,9 @@
     gbuf[j] = gsend[j]
 
     def hop(which, d, h):
+        dst = klast.at[h] if which == 0 and d == WIN else wins[which].at[2 * d + h]
         return pltpu.make_async_remote_copy(
-            src_ref=wins[which].at[2 * (d - 1) + h], dst_ref=wins[which].at[2 * d + h],
+            src_ref=wins[which].at[2 * (d - 1) + h], dst_ref=dst,
             send_sem=win_s.at[which], recv_sem=win_r.at[2 * which + h, d - 2],
             device_id=(right, j), device_id_type=MESH,
         )
@@ -210,36 +211,58 @@
             def _():
                 hop(which, WIN, h).wait_recv()
 
-    def gather(which, block, turned):
-        def step(u, carry):
-            b = u // ANC
-            slot = lax.rem(u, ANC)
-            a = anc_ref[b, slot]
-            index = 2 * (s - lax.shift_right_arithmetic(a, 1)) + (a & 1)
-            index = jnp.where(a >= 0, jnp.clip(index, 0, 2 * WIN + 1), 0)
-            rows = pl.ds(pl.multiple_of(slot * BLK, BLK), BLK)
-            entry = wins[which][index]
-            block[b, rows, :] = entry
-            turned[b, :, rows] = entry.astype(F32).T.astype(BF16)
-            return carry
-
-        lax.fori_loop(0, 2 * ANC, step, 0)
+    def window_slot(b, slot):
+        a = anc_ref[b, slot]
+        index = 2 * (s - lax.shift_right_arithmetic(a, 1)) + (a & 1)
+        return jnp.where(a >= 0, jnp.clip(index, 0, 2 * WIN + 1), 0)
+
+    def slot_rows(slot):
+        return pl.ds(pl.multiple_of(slot * BLK, BLK), BLK)
+
+    def near_keys(u, carry):
+        b, slot = u // (ANC - 2), 2 + lax.rem(u, ANC - 2)
+        kb[b, slot_rows(slot), :] = kwin[jnp.minimum(window_slot(b, slot), 2 * WIN - 1)]
+        return carry
+
+    def far_keys(u, carry):
+        b, slot = u // 2, lax.rem(u, 2)
+        index = window_slot(b, slot)
+        near = kwin[jnp.minimum(index, 2 * WIN - 1)].astype(F32)
+        far = klast[jnp.maximum(index - 2 * WIN, 0)].astype(F32)
+        kb[b, slot_rows(slot), :] = jnp.where(index >= 2 * WIN, far, near).astype(BF16)
+        return carry
+
+    def values(u, carry):
+        b, slot = u // ANC, lax.rem(u, ANC)
+        rows = slot_rows(slot)
+        entry = vwin[window_slot(b, slot)]
+        vb[b, rows, :] = entry
+        vbt[b, :, rows] = entry.astype(F32).T.astype(BF16)
+        kbt[b, :, rows] = kb[b, rows, :].astype(F32).T.astype(BF16)
+        return carry
+
+    def near_scores(p, carry):
+        i = lax.rem(j + p, KV)
+        prob[i, 2 * BLK:, :] = dot(kb[i // 4, 2 * BLK:, :], qbuf[i], NT)
+        return carry
 
     for which in range(2):
         line_copy(which, slabs[which].at[others], slabs[which].at[others], j).wait_recv()
+    line_copy(2, qsend.at[others], qbuf.at[others], j).wait_recv()
+    lax.fori_loop(0, 2 * (ANC - 2), near_keys, 0)
+    lax.fori_loop(1, KV + 1, near_scores, 0)
+    line_copy(3, gsend.at[others], gbuf.at[others], j).wait_recv()
     last_hop(0)
-    gather(0, kb, kbt)
-    line_copy(2, qsend.at[others], qbuf.at[others], j).wait_recv()
-    line_copy(3, gsend.at[others], gbuf.at[others], j).wait_recv()
+    lax.fori_loop(0, 4, far_keys, 0)
 
     def forward(p, carry):
         i = lax.rem(j + p, KV)
         b = i // 4
         slots = [slice(n * BLK, (n + 1) * BLK) for n in range(ANC)]
-        work[...] = dot(kb[b], qbuf[i], NT)
+        prob[i, :2 * BLK, :] = dot(kb[b, :2 * BLK, :], qbuf[i], NT)
 
         def score(n):
-            return work[slots[n], :] * (SCALE * LOG2E) + bias[i, slots[n], :]
+            return prob[i, slots[n], :] * (SCALE * LOG2E) + bias[i, slots[n], :]
 
         top = jnp.max(score(0), axis=0, keepdims=True)
         for n in range(1, ANC):
@@ -330,7 +353,7 @@
 
     grad_step(1, WIN)
     last_hop(1)
-    gather(1, vb, vbt)
+    lax.fori_loop(0, 2 * ANC, values, 0)
     lax.fori_loop(1, KV // 2 + 1, backward, 0)
     grad_step(1, WIN - 1)
     lax.fori_loop(KV // 2 + 1, KV + 1, backward, 0)
@@ -461,7 +484,8 @@
             pltpu.VMEM((KV, TOK, DH), BF16),
             pltpu.VMEM((KV, TOK, DH), BF16),
             rows, rows, rows, rows,
-            pltpu.VMEM((2 * WIN + 2, BLK, DH), BF16),
+            pltpu.VMEM((2 * WIN, BLK, DH), BF16),
+            pltpu.VMEM((2, BLK, DH), BF16),
             pltpu.VMEM((2 * WIN + 2, BLK, DH), BF16),
             pltpu.VMEM((2, KEYS, DH), BF16),
             pltpu.VMEM((2, KEYS, DH), BF16),

time: 81.3 us -> 79 us (0.972)
  Pallas kernels: 80.5 us -> 78.1 us
    pallas_call x1, Pallas kernels: 78.4 us -> 76 us  [body(): pl.pallas_call(functools.partial(kernel, lines), out_shape=shapes, in_spe...]
where the time goes in v4:
time: 79 us; the launch traced here: 78.8 us
  Pallas kernels  78.1 us (99%)
    pallas_call x1, Pallas kernels, body(): pl.pallas_call(functools.partial(kernel, lines), out_shape=shapes, in_spe...  76 us
    pallas_call x1, Pallas kernels, body(): pl.pallas_call(copy_kernel, out_shape=shapes, in_specs=[hbm] * 4, out_spe...  2.11 us

profile of v4, /device:TPU:25, one launch (start us, length us, event | category | flops | bytes accessed | tf_op | source)
XLA Modules:
  0.0 78.8 jit_solution(10699802663464692545)
XLA Ops:
  0.6 76.0 %shard_map.111 = (bf16[32,64,128]{2,1,0:T(8,128)(2,1)}, bf16[32,64,128]{2,1,0:T(8,128)(2,1)}, bf16[32,8,128]{2,1,0:T(8,128)(2,1)}, bf16[32,8,128]{2,1,0:T(8,128)(2,1)}) custom-call(bf16[32,64,128]{2,1,0:T(8,128)(2,1)} %q_in.1, bf16[32,8,128]{2,1,0:T(8,128)(2,1)} %k_in.1, bf16[32,8,128]{2,1,0:T(8,128)(2,1)} %v_in.1, bf16[32,64,128]{2,1,0:T(8,128)(2,1)} %g_in.1, ...), custom_call_target="tpu_custom_call" | custom-call | flops 2013265920 | bytes 4194304 | tf_op jit(solution)/shard_map/pallas_call | solution.py:467
  76.7 2.1 %shard_map.112 = (bf16[32,64,128]{2,1,0:T(8,128)(2,1)}, bf16[32,64,128]{2,1,0:T(8,128)(2,1)}, bf16[32,8,128]{2,1,0:T(8,128)(2,1)}, bf16[32,8,128]{2,1,0:T(8,128)(2,1)}) custom-call(bf16[32,64,128]{2,1,0:T(8,128)(2,1)} %get-tuple-element.8.refs_0_, bf16[32,64,128]{2,1,0:T(8,128)(2,1)} %get-tuple-element.9.refs_1_, ...), custom_call_target="tpu_custom_call" | custom-call | tf_op jit(solution)/shard_map/pallas_call | solution.py:525

commit v5 on v4

--- a/solution.py
+++ b/solution.py
@@ -37,7 +37,7 @@
     q_in, k_in, v_in, g_in, pos_in, freq_in, anc_in, end_in,
     o_out, dq_out, dk_out, dv_out,
     q_ref, k_ref, v_ref, g_ref, pos_ref, freq_ref, anc_ref, end_ref, cos_ref, sin_ref, stage, ksend, vsend, qsend, gsend, qbuf, gbuf, kwin, klast, vwin,
-    kb, vb, kbt, vbt, bias, prob, plow, work, dlow, norm, dka, dva,
+    kb, vb, kbt, vbt, bias, prob, plow, work, norm, dka, dva,
     osend, dqsend, orecv, dqrecv, tmp, gout, gin, dsend, drecv, ofin, dqfin, dkfin, dvfin,
     line_s, line_r, next_s, next_r, win_s, win_r, grad_s, grad_r, fin, load,
 ):
@@ -325,18 +325,29 @@
         factor = norm[i] * SCALE
         for n in range(ANC):
             rows = slice(n * BLK, (n + 1) * BLK)
-            dlow[rows, :] = (prob[i, rows, :] * ((work[rows, :] - inner) * factor)).astype(BF16)
-        dka[pl.ds(b * ANC, ANC)] += dot(dlow[...], qbuf[i]).reshape(ANC, BLK, DH)
-        dqsend[i] = dot(kbt[b], dlow[...]).T.astype(BF16)
+            plow[i, rows, :] = (prob[i, rows, :] * ((work[rows, :] - inner) * factor)).astype(BF16)
+        dka[pl.ds(b * ANC, ANC)] += dot(plow[i], qbuf[i]).reshape(ANC, BLK, DH)
 
         @pl.when(i != j)
         def _():
             line_copy(4, osend.at[i], orecv.at[j], i).start()
-            line_copy(5, dqsend.at[i], dqrecv.at[j], i).start()
 
         @pl.when(i == j)
         def _():
             orecv[j] = osend[i]
+
+        return carry
+
+    def query_grads(p, carry):
+        i = lax.rem(j + p, KV)
+        dqsend[i] = dot(kbt[i // 4], plow[i]).T.astype(BF16)
+
+        @pl.when(i != j)
+        def _():
+            line_copy(5, dqsend.at[i], dqrecv.at[j], i).start()
+
+        @pl.when(i == j)
+        def _():
             dqrecv[j] = dqsend[i]
 
         return carry
@@ -371,6 +382,8 @@
         grad_step(0, d)
         if d > 2:
             grad_step(1, d - 2)
+        if d == WIN - 1:
+            lax.fori_loop(1, KV + 1, query_grads, 0)
         if d in (2, 3):
             finish(3 - d)
 
@@ -495,7 +508,6 @@
             pltpu.VMEM((KV, KEYS, ROWS), F32),
             pltpu.VMEM((KV, KEYS, ROWS), BF16),
             pltpu.VMEM((KEYS, ROWS), F32),
-            pltpu.VMEM((KEYS, ROWS), BF16),
             pltpu.VMEM((KV, 1, ROWS), F32),
             pltpu.VMEM((2 * ANC + 1, BLK, DH), F32),
             pltpu.VMEM((2 * ANC + 1, BLK, DH), F32),

time: 79 us -> 79.6 us (level)
  no operation moved by 1% of the time
where the time goes in v5:
time: 79.6 us; the launch traced here: 79.4 us
  Pallas kernels  78.8 us (99%)
    pallas_call x1, Pallas kernels, body(): pl.pallas_call(functools.partial(kernel, lines), out_shape=shapes, in_spe...  76.7 us
    pallas_call x1, Pallas kernels, body(): pl.pallas_call(copy_kernel, out_shape=shapes, in_specs=[hbm] * 4, out_spe...  2.11 us

profile of v5, /device:TPU:25, one launch (start us, length us, event | category | flops | bytes accessed | tf_op | source)
XLA Modules:
  0.0 79.4 jit_solution(728633774770046789)
XLA Ops:
  0.6 76.7 %shard_map.111 = (bf16[32,64,128]{2,1,0:T(8,128)(2,1)}, bf16[32,64,128]{2,1,0:T(8,128)(2,1)}, bf16[32,8,128]{2,1,0:T(8,128)(2,1)}, bf16[32,8,128]{2,1,0:T(8,128)(2,1)}) custom-call(bf16[32,64,128]{2,1,0:T(8,128)(2,1)} %q_in.1, bf16[32,8,128]{2,1,0:T(8,128)(2,1)} %k_in.1, bf16[32,8,128]{2,1,0:T(8,128)(2,1)} %v_in.1, bf16[32,64,128]{2,1,0:T(8,128)(2,1)} %g_in.1, ...), custom_call_target="tpu_custom_call" | custom-call | flops 2013265920 | bytes 4194304 | tf_op jit(solution)/shard_map/pallas_call | solution.py:480
  77.3 2.1 %shard_map.112 = (bf16[32,64,128]{2,1,0:T(8,128)(2,1)}, bf16[32,64,128]{2,1,0:T(8,128)(2,1)}, bf16[32,8,128]{2,1,0:T(8,128)(2,1)}, bf16[32,8,128]{2,1,0:T(8,128)(2,1)}) custom-call(bf16[32,64,128]{2,1,0:T(8,128)(2,1)} %get-tuple-element.8.refs_0_, bf16[32,64,128]{2,1,0:T(8,128)(2,1)} %get-tuple-element.9.refs_1_, ...), custom_call_target="tpu_custom_call" | custom-call | tf_op jit(solution)/shard_map/pallas_call | solution.py:537
